TPU v7x, 512 devices: a whole 4x4x16 slice. The times are simulated.
512 devices in a mesh: seq: 64 (over x, z), head: 8 (over y, core).
Axes of the slice: x: 4, y: 4, z: 16, core: 2. Of those that a mesh axis runs over, the one named last changes fastest.
Arguments:
- queries: bfloat16 [8192, 16, 128], P('seq', 'head'), may hold values from -21 to 21
- seq_keys: bfloat16 [8192, 16, 128], P('seq', 'head'), may hold values from -6 to 6
- seq_values: bfloat16 [8192, 16, 128], P('seq', 'head'), may hold values from -24 to 24
- memory_keys: bfloat16 [8192, 16, 128], P('seq', 'head'), may hold values from -6 to 6
- memory_values: bfloat16 [8192, 16, 128], P('seq', 'head'), may hold values from -24 to 24
- retrieval: int32 [64, 8], P('seq'), may hold values from 0 to 63, all different within a row
- fifo_head: int32 [1], replicated, may hold values from 0 to 63
- head_gate: float32 [16], P('head'), may hold values from -2 to 2
- norm_gain: float32 [16, 128], P('head'), may hold values from 0.1 to 1.9
Outputs:
- attended: bfloat16 [8192, 16, 128], P('seq', 'head')
Inputs may be any that keep to these rules, and one draw needn't show every extreme that they name: `retrieval`: each row names 8 different memory blocks.
All inputs are finite; a program needn't handle non-finite values.
Results may differ from a plain program's by a relative error of at most 0.029.
Values may be sent and summed in bfloat16 or wider, within the bound.
No kernel may reach another device: no remote copies, remote signals or barrier semaphores. Data moves between devices by JAX's collectives and lax.ppermute only.
A program may use at most 128 MiB of HBM per device.

v0:
```python
import jax
import jax.numpy as jnp
from jax import lax
from jax.sharding import PartitionSpec as P

HEADS = 16
DH = 128
MBLK = 128
EXPIRED = 4


MASKED = -1e30


def fold_piece(softmax_state, query_rows, key_rows, value_rows, key_mask):
    old_max, old_sum, old_acc = softmax_state
    scores = jnp.einsum(
        "thd,shd->hts", query_rows, key_rows, preferred_element_type=jnp.float32
    ) * query_rows.shape[2] ** (-0.5)
    scores = jnp.where(key_mask[None], scores, MASKED)
    row_max = jnp.maximum(old_max, jnp.max(scores, -1))
    exp_scores = jnp.where(key_mask[None], jnp.exp(scores - row_max[:, :, None]), 0.0)
    new_sum = jnp.sum(exp_scores, -1)
    new_acc = jnp.einsum(
        "hts,shd->htd",
        exp_scores.astype(jnp.bfloat16),
        value_rows,
        preferred_element_type=jnp.float32,
    )
    return (row_max, new_sum, new_acc)


def on_device(
    queries,
    seq_keys,
    seq_values,
    memory_keys,
    memory_values,
    retrieval,
    fifo_head,
    head_gate,
    norm_gain,
):
    tok_rows, head_count, head_width = queries.shape
    seq_devices = lax.axis_size("seq")
    my_index = lax.axis_index("seq")
    block_count = seq_devices * tok_rows // MBLK
    query_pos = my_index * tok_rows + jnp.arange(tok_rows, dtype=jnp.int32)
    wanted = retrieval[0]
    head_pos = fifo_head[0]

    def fresh_state():
        return (
            jnp.full((head_count, tok_rows), MASKED, jnp.float32),
            jnp.zeros((head_count, tok_rows), jnp.float32),
            jnp.zeros((head_count, tok_rows, head_width), jnp.float32),
        )

    pieces = (
        lax.all_gather(seq_keys, "seq", axis=0, tiled=True),
        lax.all_gather(seq_values, "seq", axis=0, tiled=True),
    )
    key_pos = jnp.arange(pieces[0].shape[0], dtype=jnp.int32)
    local_state = fold_piece(
        fresh_state(), queries, pieces[0], pieces[1], key_pos[None, :] <= query_pos[:, None]
    )
    pieces = (
        lax.all_gather(memory_keys, "seq", axis=0, tiled=True),
        lax.all_gather(memory_values, "seq", axis=0, tiled=True),
    )
    row_count = pieces[0].shape[0]
    block_ids = jnp.arange(row_count, dtype=jnp.int32) // MBLK
    is_live = jnp.mod(block_ids - head_pos + block_count, block_count) >= EXPIRED
    block_ids, is_live = (block_ids, is_live)
    chosen = jnp.any(block_ids[:, None] == wanted[None, :], -1) & is_live
    memory_state = fold_piece(
        fresh_state(),
        queries,
        pieces[0],
        pieces[1],
        jnp.broadcast_to(chosen[None, :], (tok_rows, row_count)),
    )
    local_out = local_state[2] / local_state[1][:, :, None]
    memory_out = memory_state[2] / memory_state[1][:, :, None]
    gate_mix = jax.nn.sigmoid(head_gate)[:, None, None]
    combined = gate_mix * memory_out + (1.0 - gate_mix) * local_out
    squares = lax.psum(jnp.sum(combined * combined, axis=(0, 2)), "head")
    row_scale = lax.rsqrt(squares / (HEADS * DH) + 1e-06)
    result = combined * row_scale[None, :, None] * norm_gain[:, None, :]
    return jnp.transpose(result, (1, 0, 2)).astype(jnp.bfloat16)


def solution(mesh):
    in_specs = (
        P("seq", "head", None),
        P("seq", "head", None),
        P("seq", "head", None),
        P("seq", "head", None),
        P("seq", "head", None),
        P("seq", None),
        P(),
        P("head"),
        P("head", None),
    )
    out_specs = P("seq", "head", None)
    return jax.shard_map(
        on_device, mesh=mesh, in_specs=in_specs, out_specs=out_specs, check_vma=False
    )
```

profile of v0, /device:TPU:1, one launch (start us, length us, event | category | flops | bytes accessed | tf_op | source)
XLA Modules:
  0.0 618.5 jit_solution(12764481445013468850)
XLA Ops:
  6.5 1.5 copy.17
  8.1 0.0 all-gather.9.cloned.1.call-start
  8.1 1.5 copy.20
  9.6 0.0 all-gather.7.cloned.1.call-start
  9.7 1.6 copy.19
  11.3 1.6 copy.22
  13.6 0.8 compare_reduce_fusion
  14.4 0.7 broadcast_subtract_fusion
  15.1 0.7 iota_compare_fusion
  15.8 138.3 %all-gather.5.cloned.1.call-done = bf16[8192,2,128]{2,0,1:T(8,128)(2,1)} async-done(((bf16[128,2,128]{2,0,1:T(8,128)(2,1)}), bf16[8192,2,128]{2,0,1:T(8,128)(2,1)}) %all-gather.5.cloned.1.call-update) | async-done | bytes 4194320 | tf_op jit(solution)/shard_map/all_gather | solution.py:68
  154.1 6.8 %fusion.33 = (f32[2,128]{1,0:T(2,128)S(1)}, f32[2,128,8192]{2,1,0:T(8,128)}) fusion(bf16[8192,2,128]{2,0,1:T(8,128)(2,1)} %all-gather.5.cloned.1.call-done, bf16[128,2,128]{2,1,0:T(2,128)(2,1)} %param.9, pred[8192]{0:T(1024)(128)(4,1)S(1)} %fusion.29), kind=kOutput, calls=%fused_computation.53 | convolution fusion | flops 543162112 | bytes 12657664 | tf_op jit(solution)/shard_map/thd,shd->hts/dot_general | solution.py:17
  160.9 137.4 %all-gather.9.cloned.1.call-done = bf16[8192,2,128]{2,0,1:T(8,128)(2,1)} async-done(((bf16[128,2,128]{2,0,1:T(8,128)(2,1)}), bf16[8192,2,128]{2,0,1:T(8,128)(2,1)}) %all-gather.9.cloned.1.call-update) | async-done | bytes 4194320 | tf_op jit(solution)/shard_map/all_gather | solution.py:60
  298.3 4.5 fusion.32
  302.8 0.1 copy-done.1
  303.0 1.8 fusion.2
  304.8 1.3 copy-done
  306.0 2.1 fusion.4
  308.2 132.3 %all-gather.7.cloned.1.call-done = bf16[8192,2,128]{0,2,1:T(8,128)(2,1)} async-done(((bf16[128,2,128]{0,2,1:T(8,128)(2,1)}), bf16[8192,2,128]{0,2,1:T(8,128)(2,1)}) %all-gather.7.cloned.1.call-update) | async-done | bytes 4194320 | tf_op jit(solution)/shard_map/all_gather | solution.py:69
  440.5 6.0 fusion.8
  446.5 136.7 %all-gather.11.cloned.1.call-done = bf16[8192,2,128]{0,2,1:T(8,128)(2,1)} async-done(((bf16[128,2,128]{0,2,1:T(8,128)(2,1)}), bf16[8192,2,128]{0,2,1:T(8,128)(2,1)}) %all-gather.11.cloned.1.call-update) | async-done | bytes 4194320 | tf_op jit(solution)/shard_map/all_gather | solution.py:61
  583.2 6.3 %multiply_reduce_fusion = (f32[128]{0:T(128)S(1)}, f32[2,128,128]{1,2,0:T(8,128)S(1)}) fusion(f32[2,128,128]{1,2,0:T(8,128)S(1)} %fusion.8, f32[2,128]{1,0:T(2,128)S(1)} %fusion.4, f32[2]{0:T(128)S(1)} %get-tuple-element.5, f32[2,128]{1,0:T(2,128)S(1)} %fusion.2, f32[2]{0:T(128)S(1)} %get-tuple-element.6, ...), kind=kOutput, calls=%fused_computation.27 | convolution fusion | flops 543391616 | bytes 13897232 | tf_op jit(solution)/shard_map/hts,shd->htd/dot_general | solution.py:24
  589.5 21.6 %psum.7 = f32[128]{0:T(128)S(1)} all-reduce(f32[128]{0:T(128)S(1)} %get-tuple-element.11), channel_id=1, replica_groups=mesh['seq'=64,'head'=8] {'head'}, use_global_device_ids=true, to_apply=%region_6.7 | all-reduce | flops 128 | bytes 1024 | tf_op jit(solution)/shard_map/psum | solution.py:87
  611.1 0.1 fusion.21
  611.2 0.8 copy.23
  (18 shorter events, 0.2 us)
Async XLA Ops:
  6.5 291.8 %copy-start.2 = (bf16[128,2,128]{2,1,0:T(2,128)(2,1)S(1)}, bf16[128,2,128]{2,1,0:T(2,128)(2,1)}, u32[]{:S(2)}) copy-start(bf16[128,2,128]{2,1,0:T(2,128)(2,1)} %param.9) | copy-start | bytes 196612
  6.5 147.6 %all-gather.5.cloned.1.call-start = ((), (), s32[]{:S(2)}) async-start(), calls=%async_computation | async-start | bytes 4259840 | tf_op jit(solution)/shard_map/all_gather | solution.py:68
  8.1 290.3 %all-gather.9.cloned.1.call-start = ((), (), s32[]{:S(2)}) async-start(), calls=%async_computation.2 | async-start | bytes 4259840 | tf_op jit(solution)/shard_map/all_gather | solution.py:60
  9.6 430.9 %all-gather.7.cloned.1.call-start = ((), (), s32[]{:S(2)}) async-start(), calls=%async_computation.1 | async-start | bytes 4259840 | tf_op jit(solution)/shard_map/all_gather | solution.py:69
  11.3 571.9 %all-gather.11.cloned.1.call-start = ((), (), s32[]{:S(2)}) async-start(), calls=%async_computation.3 | async-start | bytes 4259840 | tf_op jit(solution)/shard_map/all_gather | solution.py:61
  298.3 4.6 copy-start.1
  302.8 3.2 copy-start
  583.2 28.0 %copy-start.3 = (f32[2,128]{1,0:T(2,128)S(1)}, f32[2,128]{1,0:T(2,128)}, u32[]{:S(2)}) copy-start(f32[2,128]{1,0:T(2,128)} %param.17) | copy-start | bytes 3076
Sparse Core Ops, SparseCore 0:
  10.3 143.7 all-gather.4
  157.1 141.2 all-gather.8
  301.2 139.1 all-gather.6
  443.2 139.8 all-gather.10
where the time goes:
time: 619 us
  waiting for transfers between devices  545 us (88%)
  matrix products  23.6 us (4%)
  blocking collectives  21.6 us (3%)
  between operations  13.8 us (2%)
  local copies, waits for them, and re-layouts  8.29 us (1%)
  other arithmetic  6.25 us (1%)
    all_gather x1, waiting for transfers between devices, on_device(): lax.all_gather(memory_keys, 'seq', axis=0, tiled=True)  138 us
    all_gather x1, waiting for transfers between devices, on_device(): lax.all_gather(seq_keys, 'seq', axis=0, tiled=True)  137 us
    all_gather x1, waiting for transfers between devices, on_device(): lax.all_gather(seq_values, 'seq', axis=0, tiled=True)  137 us
    all_gather x1, waiting for transfers between devices, on_device(): lax.all_gather(memory_values, 'seq', axis=0, tiled=True)  132 us
    psum x1, blocking collectives, on_device(): squares = lax.psum(jnp.sum(combined * combined, axis=(0, 2)), 'head')  21.6 us
  transfers between devices with their start and end apart: 4, of which 4 were waited for; matrix products, arithmetic and copies ran while one was open for 5% of the time, Pallas kernels for 0%

commit v1 on v0

v1 whole, which is shorter than its diff:
```python
import jax
import jax.numpy as jnp
from jax import lax
from jax.experimental import pallas as pl
from jax.experimental.pallas import tpu as pltpu
from jax.sharding import PartitionSpec as P

HEADS = 16
DH = 128
TOK = 128
EXPIRED = 4
BLOCKS = 64
NX, NZ = 4, 16
NR = 8
NC = 8
QROWS = 2 * TOK + 16
OROWS = 4 * DH + 16
NEG = -1e30
FLOOR = -1e29
LOG2_SCALE = DH**-0.5 * 1.4426950408889634

R_GROUPS = [[x * NZ + 2 * r + par for r in range(NR)] for x in range(NX) for par in range(2)]
C_GROUPS = [[x * NZ + 2 * k + par for x in range(NX) for par in range(2)] for k in range(NZ // 2)]

NT = (((1,), (1,)), ((), ()))
NN = (((1,), (0,)), ((), ()))


def dot(a, b, dims):
    return lax.dot_general(a, b, dims, preferred_element_type=jnp.float32)


def split_perm():
    row = lax.broadcasted_iota(jnp.int32, (2 * TOK, 2 * TOK), 0)
    col = lax.broadcasted_iota(jnp.int32, (2 * TOK, 2 * TOK), 1)
    source = (row % TOK) * 2 + row // TOK
    return jnp.where(col == source, 1.0, 0.0).astype(jnp.bfloat16)


def prep_kernel(want_ref, fifo_ref, q_ref, k_ref, v_ref, mk_ref, mv_ref, kv_out, q_out):
    perm = split_perm()
    for place, ref in ((0, k_ref), (2, mk_ref)):
        kv_out[pl.ds(place * 256, 256), :] = dot(perm, ref[...], NN).astype(jnp.bfloat16)
    for place, ref in ((1, v_ref), (3, mv_ref)):
        rows = dot(perm, ref[...], NN)
        for h in range(2):
            block = jnp.transpose(rows[h * TOK : (h + 1) * TOK, :])
            kv_out[pl.ds(place * 256 + h * TOK, TOK), :] = block.astype(jnp.bfloat16)
    q_rows = dot(perm, q_ref[...], NN).astype(jnp.bfloat16)
    row = lax.broadcasted_iota(jnp.int32, (16, TOK), 0)
    for c in range(NC):
        q_out[c, pl.ds(0, 2 * TOK), :] = q_rows
        block = (c // 2) * NZ + 2 * row + c % 2
        chosen = block == want_ref[0, 0]
        for i in range(1, 8):
            chosen = chosen | (block == want_ref[0, i])
        live = ((block - fifo_ref[0] + BLOCKS) & (BLOCKS - 1)) >= EXPIRED
        q_out[c, pl.ds(2 * TOK, 16), :] = jnp.where(chosen & live, 0.0, NEG).astype(jnp.bfloat16)


def attend_kernel(pos_ref, q_ref, kv_ref, out_ref):
    my_x, my_pair, my_par = pos_ref[0], pos_ref[1], pos_ref[2]
    ahead = lax.broadcasted_iota(jnp.int32, (TOK, 2 * TOK), 0) - lax.broadcasted_iota(
        jnp.int32, (TOK, 2 * TOK), 1
    )

    def step(xq, carry):
        stats = []
        extra = [q_ref[2 * xq + par, pl.ds(2 * TOK, 16), :].astype(jnp.float32) for par in range(2)]
        bias = jnp.concatenate(extra, 1)
        for kind in range(2):
            for h in range(2):
                q_rows = jnp.concatenate(
                    [q_ref[2 * xq + par, pl.ds(h * TOK, TOK), :] for par in range(2)], 0
                )
                scores = []
                for r in range(NR):
                    keys = kv_ref[r, pl.ds(kind * 512 + h * TOK, TOK), :]
                    s = dot(keys, q_rows, NT)
                    if kind == 0:
                        gap = ((xq - my_x) * NZ + 2 * my_pair - 2 * r - my_par) * TOK
                        s = jnp.where(ahead <= gap, s, NEG)
                    else:
                        s = s + bias[r : r + 1, :]
                    scores.append(s)
                s = jnp.concatenate(scores, 0)
                top = jnp.maximum(jnp.max(s, 0, keepdims=True), FLOOR) * LOG2_SCALE
                e = jnp.exp2(s * LOG2_SCALE - top)
                total = jnp.sum(e, 0, keepdims=True)
                total = jnp.maximum(total, 1e-30)
                vals = jnp.concatenate(
                    [kv_ref[r, pl.ds(kind * 512 + 256 + h * TOK, TOK), :] for r in range(NR)], 1
                )
                acc = dot(vals, e.astype(jnp.bfloat16), NN) * (1.0 / total)
                acc = acc.astype(jnp.bfloat16)
                for par in range(2):
                    out_ref[2 * xq + par, pl.ds((kind * 2 + h) * DH, DH), :] = acc[
                        :, par * TOK : (par + 1) * TOK
                    ]
                lse = top + jnp.log2(total)
                for _ in range(3):
                    part = lse.astype(jnp.bfloat16).astype(jnp.float32)
                    stats.append(part)
                    lse = lse - part
        stats.append(jnp.zeros((4, 2 * TOK), jnp.float32))
        tile = jnp.concatenate(stats, 0).astype(jnp.bfloat16)
        for par in range(2):
            out_ref[2 * xq + par, pl.ds(4 * DH, 16), :] = tile[:, par * TOK : (par + 1) * TOK]
        return carry

    lax.fori_loop(0, NX, step, 0)


def merge_kernel(gate_ref, part_ref, comb_ref, sq_ref):
    stats = [part_ref[c, pl.ds(4 * DH, 16), :].astype(jnp.float32) for c in range(NC)]
    squares = jnp.zeros((1, TOK), jnp.float32)
    for h in range(2):
        merged = []
        for kind in range(2):
            at = (kind * 2 + h) * 3
            lse = [st[at : at + 1] + st[at + 1 : at + 2] + st[at + 2 : at + 3] for st in stats]
            top = lse[0]
            for one in lse[1:]:
                top = jnp.maximum(top, one)
            weight = [jnp.exp2(one - top) for one in lse]
            total = weight[0]
            for one in weight[1:]:
                total = total + one
            acc = jnp.zeros((DH, TOK), jnp.float32)
            for c in range(NC):
                rows = part_ref[c, pl.ds((kind * 2 + h) * DH, DH), :].astype(jnp.float32)
                acc = acc + rows * weight[c]
            merged.append(acc * (1.0 / total))
        gate = gate_ref[h : h + 1, :]
        comb = gate * merged[1] + (1.0 - gate) * merged[0]
        comb_ref[h] = comb
        squares = squares + jnp.sum(comb * comb, 0, keepdims=True)
    sq_ref[...] = jnp.broadcast_to(squares, (8, TOK))


def final_kernel(sq_ref, comb_ref, gain_ref, out_ref):
    mean_square = jnp.sum(sq_ref[...], 0, keepdims=True) * (1.0 / (HEADS * DH))
    scale = lax.rsqrt(mean_square + 1e-06)
    diag = lax.broadcasted_iota(jnp.int32, (DH, DH), 0) == lax.broadcasted_iota(jnp.int32, (DH, DH), 1)
    cols = []
    for h in range(2):
        gain = jnp.sum(jnp.where(diag, gain_ref[h : h + 1, :], 0.0), 1, keepdims=True)
        cols.append((comb_ref[h] * scale * gain).astype(jnp.bfloat16))
    row = lax.broadcasted_iota(jnp.int32, (2 * TOK, 2 * TOK), 0)
    col = lax.broadcasted_iota(jnp.int32, (2 * TOK, 2 * TOK), 1)
    pick = jnp.where(col == (row % 2) * TOK + row // 2, 1.0, 0.0).astype(jnp.bfloat16)
    out_ref[...] = dot(pick, jnp.concatenate(cols, 1), NT).astype(jnp.bfloat16)


VMEM = pl.BlockSpec(memory_space=pltpu.VMEM)
SMEM = pl.BlockSpec(memory_space=pltpu.SMEM)
PARAMS = pltpu.CompilerParams(vmem_limit_bytes=40 * 2**20)


def on_device(queries, seq_keys, seq_values, memory_keys, memory_values, retrieval, fifo_head, head_gate, norm_gain):
    me = lax.axis_index("seq")
    pos = jnp.stack([me // NZ, (me % NZ) // 2, me % 2]).astype(jnp.int32)
    flat = lambda a: a.reshape(2 * TOK, DH)
    kv, q_parts = pl.pallas_call(
        prep_kernel,
        out_shape=(
            jax.ShapeDtypeStruct((1024, DH), jnp.bfloat16),
            jax.ShapeDtypeStruct((NC, QROWS, DH), jnp.bfloat16),
        ),
        in_specs=[SMEM, SMEM] + [VMEM] * 5,
        out_specs=(VMEM, VMEM),
        compiler_params=PARAMS,
        name="prep",
    )(retrieval, fifo_head, *map(flat, (queries, seq_keys, seq_values, memory_keys, memory_values)))
    kv_all = lax.all_gather(kv, "seq", axis_index_groups=R_GROUPS)
    q_all = lax.all_to_all(q_parts, "seq", 0, 0, axis_index_groups=C_GROUPS, tiled=True)
    parts = pl.pallas_call(
        attend_kernel,
        out_shape=jax.ShapeDtypeStruct((NC, OROWS, DH), jnp.bfloat16),
        in_specs=[SMEM, VMEM, VMEM],
        out_specs=VMEM,
        compiler_params=PARAMS,
        name="attend",
    )(pos, q_all, kv_all)
    parts = lax.all_to_all(parts, "seq", 0, 0, axis_index_groups=C_GROUPS, tiled=True)
    gate = jnp.broadcast_to(jax.nn.sigmoid(head_gate)[:, None], (2, TOK))
    comb, squares = pl.pallas_call(
        merge_kernel,
        out_shape=(
            jax.ShapeDtypeStruct((2, DH, TOK), jnp.float32),
            jax.ShapeDtypeStruct((8, TOK), jnp.float32),
        ),
        in_specs=[VMEM, VMEM],
        out_specs=(VMEM, VMEM),
        compiler_params=PARAMS,
        name="merge",
    )(gate, parts)
    squares = lax.all_to_all(squares, "head", 0, 0, tiled=True)
    out = pl.pallas_call(
        final_kernel,
        out_shape=jax.ShapeDtypeStruct((2 * TOK, DH), jnp.bfloat16),
        in_specs=[VMEM] * 3,
        out_specs=VMEM,
        compiler_params=PARAMS,
        name="final",
    )(squares, comb, norm_gain)
    return out.reshape(TOK, 2, DH)


def solution(mesh):
    in_specs = (P("seq", "head", None),) * 5 + (P("seq", None), P(), P("head"), P("head", None))
    return jax.shard_map(
        on_device, mesh=mesh, in_specs=in_specs, out_specs=P("seq", "head", None), check_vma=False
    )
```

time: 619 us -> 134 us (0.22)
  waiting for transfers between devices: 545 us -> 76.7 us
  matrix products: 23.6 us -> 0 us
  Pallas kernels: 0 us -> 13.3 us
  starting transfers between devices: 0.13 us -> 10.7 us
  blocking collectives: 21.6 us -> 11.7 us
    all_gather x4 -> x1, waiting for transfers between devices: 545 us -> 55.1 us  [on_device(): kv_all = lax.all_gather(kv, 'seq', axis_index_groups=R_GROUPS)]
    dot_general x4 -> x0, matrix products: 23.6 us -> none  [the longest x2 12.3 us: fold_piece(): jnp.einsum('hts,shd->htd', exp_scores.astype(jnp.bfloat16), value_rows, p...]
    psum x1 -> x0, blocking collectives: 21.6 us -> none  [on_device(): squares = lax.psum(jnp.sum(combined * combined, axis=(0, 2)), 'head')]
    all_to_all x0 -> x2, waiting for transfers between devices: none -> 21.6 us  [the longest x1 14 us: on_device(): lax.all_to_all(parts, 'seq', 0, 0, axis_index_groups=C_GROUPS, tiled=True)]
    pallas_call x0 -> x4, Pallas kernels: none -> 13.3 us  [the longest x1 10.3 us: on_device(): pl.pallas_call(attend_kernel, out_shape=jax.ShapeDtypeStruct((NC, OROWS,...]
    all_to_all x0 -> x1, blocking collectives: none -> 11.7 us  [on_device(): squares = lax.all_to_all(squares, 'head', 0, 0, tiled=True)]
    all_to_all x0 -> x2, starting transfers between devices: none -> 10.7 us  [the longest x1 6.23 us: on_device(): lax.all_to_all(q_parts, 'seq', 0, 0, axis_index_groups=C_GROUPS, tiled=True)]
  transfers between devices with their start and end apart: 4 -> 3, of which waited for: 4 -> 3; matrix products, arithmetic and copies ran while one was open for 5% -> 0% of each run, Pallas kernels for 0% -> 0%
where the time goes in v1:
time: 134 us; the launch traced here: 133 us
  waiting for transfers between devices  76.7 us (57%)
  between operations  14.1 us (11%)
  Pallas kernels  13.3 us (10%)
  blocking collectives  11.7 us (9%)
  starting transfers between devices  10.7 us (8%)
  local copies, waits for them, and re-layouts  6.51 us (5%)
    all_gather x1, waiting for transfers between devices, on_device(): kv_all = lax.all_gather(kv, 'seq', axis_index_groups=R_GROUPS)  55.1 us
    all_to_all x1, waiting for transfers between devices, on_device(): lax.all_to_all(parts, 'seq', 0, 0, axis_index_groups=C_GROUPS, tiled=True)  14 us
    all_to_all x1, blocking collectives, on_device(): squares = lax.all_to_all(squares, 'head', 0, 0, tiled=True)  11.7 us
    pallas_call x1, Pallas kernels, on_device(): pl.pallas_call(attend_kernel, out_shape=jax.ShapeDtypeStruct((NC, OROWS,...  10.3 us
    all_to_all x1, waiting for transfers between devices, on_device(): lax.all_to_all(q_parts, 'seq', 0, 0, axis_index_groups=C_GROUPS, tiled=True)  7.64 us
    unnamed x18, local copies, waits for them, and re-layouts  6.44 us
    all_to_all x1, starting transfers between devices, on_device(): lax.all_to_all(q_parts, 'seq', 0, 0, axis_index_groups=C_GROUPS, tiled=True)  6.23 us
    all_to_all x1, starting transfers between devices, on_device(): lax.all_to_all(parts, 'seq', 0, 0, axis_index_groups=C_GROUPS, tiled=True)  4.48 us
  transfers between devices with their start and end apart: 3, of which 3 were waited for; matrix products, arithmetic and copies ran while one was open for 0% of the time, Pallas kernels for 0%

profile of v1, /device:TPU:1, one launch (start us, length us, event | category | flops | bytes accessed | tf_op | source)
XLA Modules:
  0.0 133.1 jit_solution(16385762723754316454)
XLA Ops:
  6.5 0.0 all-gather.3.cloned.1.call-start
  7.2 0.0 copy-start.1
  7.2 0.8 copy-done.1
  8.0 0.8 copy-done.2
  8.9 0.8 copy-done.3
  9.7 0.8 copy-done.4
  10.6 0.8 copy-done.5
  11.4 0.7 copy-done.7
  12.0 1.9 %prep.1 = (bf16[1024,128]{1,0:T(8,128)(2,1)}, bf16[8,272,128]{2,1,0:T(8,128)(2,1)}) custom-call(s32[1,8]{1,0:T(1,128)S(1)} %copy-done.7, s32[1]{0:T(128)S(6)} %copy.11.fifo_ref, bf16[256,128]{1,0:T(8,128)(2,1)S(1)} %bitcast.15, bf16[256,128]{1,0:T(8,128)(2,1)S(1)} %bitcast.16, bf16[256,128]{1,0:T(8,128)(2,1)S(1)} %bitcast.17, bf16[256,128]{1,0:T(8,128)(2,1)S(1)} %bitcast.18, ...), custom_call_target="tpu_custom_call" | custom-call | tf_op jit(solution)/shard_map/prep/pallas_call | solution.py:164
  13.9 0.0 all-gather.3.cloned.1.call-update
  13.9 6.2 %all-to-all-start = ((bf16[8,272,128]{2,1,0:T(8,128)(2,1)}), bf16[8,272,128]{2,1,0:T(8,128)(2,1)S(1)}, u32[]{:S(2)}, u32[]{:S(2)}) async-start(bf16[8,272,128]{2,1,0:T(8,128)(2,1)} %get-tuple-element.9), calls=%async_computation | async-start | bytes 1114112 | tf_op jit(solution)/shard_map/all_to_all | solution.py:176
  20.2 0.1 pad_add_fusion.pos_ref
  20.2 7.6 %all-to-all-done.q_ref = bf16[8,272,128]{2,1,0:T(8,128)(2,1)S(1)} async-done(((bf16[8,272,128]{2,1,0:T(8,128)(2,1)}), bf16[8,272,128]{2,1,0:T(8,128)(2,1)S(1)}, u32[]{:S(2)}, u32[]{:S(2)}) %all-to-all-start) | async-done | bytes 557088 | tf_op jit(solution)/shard_map/all_to_all | solution.py:176
  27.9 55.1 %all-gather.3.cloned.1.call-done = bf16[8192,128]{1,0:T(8,128)(2,1)} async-done(((bf16[1024,128]{1,0:T(8,128)(2,1)}), bf16[8192,128]{1,0:T(8,128)(2,1)}) %all-gather.3.cloned.1.call-update) | async-done | bytes 2097168 | tf_op jit(solution)/shard_map/all_gather | solution.py:175
  83.0 1.6 %copy-done = bf16[8192,128]{1,0:T(8,128)(2,1)S(1)} copy-done((bf16[8192,128]{1,0:T(8,128)(2,1)S(1)}, bf16[8192,128]{1,0:T(8,128)(2,1)}, u32[]{:S(2)}) %copy-start) | copy-done | bytes 2097176
  84.5 10.3 %attend.1 = bf16[8,528,128]{2,1,0:T(8,128)(2,1)} custom-call(s32[3]{0:T(128)S(1)} %pad_add_fusion.pos_ref, bf16[8,272,128]{2,1,0:T(8,128)(2,1)S(1)} %all-to-all-done.q_ref, bf16[8,1024,128]{2,1,0:T(8,128)(2,1)S(1)} %bitcast.14), custom_call_target="tpu_custom_call" | custom-call | tf_op jit(solution)/shard_map/attend/pallas_call | solution.py:177
  94.8 4.5 %all-to-all-start.1 = ((bf16[8,528,128]{2,1,0:T(8,128)(2,1)}), bf16[8,528,128]{2,1,0:T(8,128)(2,1)S(1)}, u32[]{:S(2)}, u32[]{:S(2)}) async-start(bf16[8,528,128]{2,1,0:T(8,128)(2,1)} %attend.1), calls=%async_computation.1 | async-start | bytes 2162688 | tf_op jit(solution)/shard_map/all_to_all | solution.py:185
  99.3 0.0 copy-done.8
  99.3 0.0 copy-start.6
  99.3 14.0 %all-to-all-done.1.part_ref = bf16[8,528,128]{2,1,0:T(8,128)(2,1)S(1)} async-done(((bf16[8,528,128]{2,1,0:T(8,128)(2,1)}), bf16[8,528,128]{2,1,0:T(8,128)(2,1)S(1)}, u32[]{:S(2)}, u32[]{:S(2)}) %all-to-all-start.1) | async-done | bytes 1081376 | tf_op jit(solution)/shard_map/all_to_all | solution.py:185
  113.3 0.1 broadcast_in_dim.2.gate_ref
  113.4 0.3 merge.1
  113.7 11.7 %all_to_all.21 = f32[8,1,128]{2,1,0:T(1,128)S(1)} all-to-all(f32[8,1,128]{2,1,0:T(1,128)S(1)} %bitcast.21), channel_id=1, replica_groups=mesh['seq'=64,'head'=8] {'head'}, dimensions={0} | all-to-all | bytes 8192 | tf_op jit(solution)/shard_map/all_to_all | solution.py:198
  125.3 0.9 final.1
  (9 shorter events, 0.0 us)
Async XLA Ops:
  6.5 76.4 %all-gather.3.cloned.1.call-start = ((), (), s32[]{:S(2)}) async-start(), calls=%async_computation.3 | async-start | bytes 2359296 | tf_op jit(solution)/shard_map/all_gather | solution.py:175
  7.2 0.8 copy-start.1
  8.0 0.8 copy-start.2
  8.9 0.8 copy-start.3
  9.7 0.8 copy-start.4
  10.5 0.8 copy-start.5
  11.4 0.7 copy-start.7
  13.9 13.9 %all-to-all-start = ((bf16[8,272,128]{2,1,0:T(8,128)(2,1)}), bf16[8,272,128]{2,1,0:T(8,128)(2,1)S(1)}, u32[]{:S(2)}, u32[]{:S(2)}) async-start(bf16[8,272,128]{2,1,0:T(8,128)(2,1)} %get-tuple-element.9), calls=%async_computation | async-start | bytes 1114112 | tf_op jit(solution)/shard_map/all_to_all | solution.py:176
  83.0 1.6 %copy-start = (bf16[8192,128]{1,0:T(8,128)(2,1)S(1)}, bf16[8192,128]{1,0:T(8,128)(2,1)}, u32[]{:S(2)}) copy-start(bf16[8192,128]{1,0:T(8,128)(2,1)} %all-gather.3.cloned.1.call-done) | copy-start | bytes 6291460
  94.8 4.5 %copy-start.8 = (f32[2]{0:T(128)S(1)}, f32[2]{0:T(128)}, u32[]{:S(2)}) copy-start(f32[2]{0:T(128)} %param.16) | copy-start | bytes 28
  94.8 18.5 %all-to-all-start.1 = ((bf16[8,528,128]{2,1,0:T(8,128)(2,1)}), bf16[8,528,128]{2,1,0:T(8,128)(2,1)S(1)}, u32[]{:S(2)}, u32[]{:S(2)}) async-start(bf16[8,528,128]{2,1,0:T(8,128)(2,1)} %attend.1), calls=%async_computation.1 | async-start | bytes 2162688 | tf_op jit(solution)/shard_map/all_to_all | solution.py:185
  99.3 26.0 %copy-start.6 = (f32[2,128]{1,0:T(2,128)S(1)}, f32[2,128]{1,0:T(2,128)}, u32[]{:S(2)}) copy-start(f32[2,128]{1,0:T(2,128)} %gain_ref.1) | copy-start | bytes 3076
Sparse Core Ops, SparseCore 0:
  14.0 68.8 all-gather.2

commit v2 on v1

--- a/solution.py
+++ b/solution.py
@@ -15,6 +15,7 @@
 NC = 8
 QROWS = 2 * TOK + 16
 OROWS = 4 * DH + 16
+KVROWS = 8 * TOK + 16
 NEG = -1e30
 FLOOR = -1e29
 LOG2_SCALE = DH**-0.5 * 1.4426950408889634
@@ -37,28 +38,73 @@
     return jnp.where(col == source, 1.0, 0.0).astype(jnp.bfloat16)
 
 
-def prep_kernel(want_ref, fifo_ref, q_ref, k_ref, v_ref, mk_ref, mv_ref, kv_out, q_out):
+def query_kernel(want_hbm, fifo_hbm, q_hbm, q_out, want, fifo, q_in, sems):
+    copies = [
+        pltpu.make_async_copy(src, dst, sems.at[i])
+        for i, (src, dst) in enumerate(((want_hbm, want), (fifo_hbm, fifo), (q_hbm, q_in)))
+    ]
+    for copy in copies:
+        copy.start()
     perm = split_perm()
-    for place, ref in ((0, k_ref), (2, mk_ref)):
-        kv_out[pl.ds(place * 256, 256), :] = dot(perm, ref[...], NN).astype(jnp.bfloat16)
-    for place, ref in ((1, v_ref), (3, mv_ref)):
-        rows = dot(perm, ref[...], NN)
-        for h in range(2):
-            block = jnp.transpose(rows[h * TOK : (h + 1) * TOK, :])
-            kv_out[pl.ds(place * 256 + h * TOK, TOK), :] = block.astype(jnp.bfloat16)
-    q_rows = dot(perm, q_ref[...], NN).astype(jnp.bfloat16)
+    for copy in copies:
+        copy.wait()
+    q_rows = dot(perm, q_in[...], NN).astype(jnp.bfloat16)
     row = lax.broadcasted_iota(jnp.int32, (16, TOK), 0)
     for c in range(NC):
         q_out[c, pl.ds(0, 2 * TOK), :] = q_rows
         block = (c // 2) * NZ + 2 * row + c % 2
-        chosen = block == want_ref[0, 0]
+        chosen = block == want[0, 0]
         for i in range(1, 8):
-            chosen = chosen | (block == want_ref[0, i])
-        live = ((block - fifo_ref[0] + BLOCKS) & (BLOCKS - 1)) >= EXPIRED
+            chosen = chosen | (block == want[0, i])
+        live = ((block - fifo[0] + BLOCKS) & (BLOCKS - 1)) >= EXPIRED
         q_out[c, pl.ds(2 * TOK, 16), :] = jnp.where(chosen & live, 0.0, NEG).astype(jnp.bfloat16)
 
 
-def attend_kernel(pos_ref, q_ref, kv_ref, out_ref):
+def code_kernel(k_hbm, v_hbm, mk_hbm, mv_hbm, kv_out, rows_in, sems):
+    copies = [
+        pltpu.make_async_copy(src, rows_in.at[i], sems.at[i])
+        for i, src in enumerate((k_hbm, v_hbm, mk_hbm, mv_hbm))
+    ]
+    for copy in copies:
+        copy.start()
+    perm = split_perm()
+    powers = []
+    for i, copy in enumerate(copies):
+        copy.wait()
+        rows = dot(perm, rows_in[i], NN)
+        for h in range(2):
+            block = rows[h * TOK : (h + 1) * TOK, :]
+            if i % 2:
+                block = jnp.transpose(block)
+            peak = jnp.max(jnp.max(jnp.abs(block), 0, keepdims=True), 1, keepdims=True)
+            power = jnp.floor(14.999 - jnp.log2(jnp.maximum(peak, 1e-30)))
+            power = jnp.broadcast_to(power, (1, TOK))
+            code = jnp.floor(block * jnp.exp2(power) + 0.5).astype(jnp.int32)
+            kv_out[pl.ds((i * 2 + h) * TOK, TOK), :] = code.astype(jnp.int16)
+            powers.append(power)
+    powers.append(jnp.zeros((8, TOK), jnp.float32))
+    tile = jnp.concatenate(powers, 0).astype(jnp.int32)
+    kv_out[pl.ds(8 * TOK, 16), :] = tile.astype(jnp.int16)
+
+
+def decode(kv_ref, keys_ref, vals_ref):
+    for r in range(NR):
+        power = kv_ref[r, pl.ds(8 * TOK, 16), :].astype(jnp.int32).astype(jnp.float32)
+        factor = jnp.exp2(-power)
+        for i in range(4):
+            for h in range(2):
+                code = kv_ref[r, pl.ds((i * 2 + h) * TOK, TOK), :].astype(jnp.int32)
+                block = code.astype(jnp.float32) * factor[i * 2 + h : i * 2 + h + 1, :]
+                block = block.astype(jnp.bfloat16)
+                at = (i // 2) * 2 + h
+                if i % 2:
+                    vals_ref[at, :, pl.ds(r * TOK, TOK)] = block
+                else:
+                    keys_ref[at, pl.ds(r * TOK, TOK), :] = block
+
+
+def attend_kernel(pos_ref, q_ref, kv_ref, out_ref, keys_ref, vals_ref):
+    decode(kv_ref, keys_ref, vals_ref)
     my_x, my_pair, my_par = pos_ref[0], pos_ref[1], pos_ref[2]
     ahead = lax.broadcasted_iota(jnp.int32, (TOK, 2 * TOK), 0) - lax.broadcasted_iota(
         jnp.int32, (TOK, 2 * TOK), 1
@@ -75,7 +121,7 @@
                 )
                 scores = []
                 for r in range(NR):
-                    keys = kv_ref[r, pl.ds(kind * 512 + h * TOK, TOK), :]
+                    keys = keys_ref[kind * 2 + h, pl.ds(r * TOK, TOK), :]
                     s = dot(keys, q_rows, NT)
                     if kind == 0:
                         gap = ((xq - my_x) * NZ + 2 * my_pair - 2 * r - my_par) * TOK
@@ -88,10 +134,7 @@
                 e = jnp.exp2(s * LOG2_SCALE - top)
                 total = jnp.sum(e, 0, keepdims=True)
                 total = jnp.maximum(total, 1e-30)
-                vals = jnp.concatenate(
-                    [kv_ref[r, pl.ds(kind * 512 + 256 + h * TOK, TOK), :] for r in range(NR)], 1
-                )
-                acc = dot(vals, e.astype(jnp.bfloat16), NN) * (1.0 / total)
+                acc = dot(vals_ref[kind * 2 + h], e.astype(jnp.bfloat16), NN) * (1.0 / total)
                 acc = acc.astype(jnp.bfloat16)
                 for par in range(2):
                     out_ref[2 * xq + par, pl.ds((kind * 2 + h) * DH, DH), :] = acc[
@@ -153,6 +196,7 @@
 
 
 VMEM = pl.BlockSpec(memory_space=pltpu.VMEM)
+ANY = pl.BlockSpec(memory_space=pl.ANY)
 SMEM = pl.BlockSpec(memory_space=pltpu.SMEM)
 PARAMS = pltpu.CompilerParams(vmem_limit_bytes=40 * 2**20)
 
@@ -161,24 +205,43 @@
     me = lax.axis_index("seq")
     pos = jnp.stack([me // NZ, (me % NZ) // 2, me % 2]).astype(jnp.int32)
     flat = lambda a: a.reshape(2 * TOK, DH)
-    kv, q_parts = pl.pallas_call(
-        prep_kernel,
-        out_shape=(
-            jax.ShapeDtypeStruct((1024, DH), jnp.bfloat16),
-            jax.ShapeDtypeStruct((NC, QROWS, DH), jnp.bfloat16),
-        ),
-        in_specs=[SMEM, SMEM] + [VMEM] * 5,
-        out_specs=(VMEM, VMEM),
-        compiler_params=PARAMS,
-        name="prep",
-    )(retrieval, fifo_head, *map(flat, (queries, seq_keys, seq_values, memory_keys, memory_values)))
+    q_parts = pl.pallas_call(
+        query_kernel,
+        out_shape=jax.ShapeDtypeStruct((NC, QROWS, DH), jnp.bfloat16),
+        in_specs=[ANY] * 3,
+        out_specs=VMEM,
+        scratch_shapes=[
+            pltpu.SMEM((1, 8), jnp.int32),
+            pltpu.SMEM((1,), jnp.int32),
+            pltpu.VMEM((2 * TOK, DH), jnp.bfloat16),
+            pltpu.SemaphoreType.DMA((3,)),
+        ],
+        compiler_params=PARAMS,
+        name="query",
+    )(retrieval, fifo_head, flat(queries))
+    q_all = lax.all_to_all(q_parts, "seq", 0, 0, axis_index_groups=C_GROUPS, tiled=True)
+    kv = pl.pallas_call(
+        code_kernel,
+        out_shape=jax.ShapeDtypeStruct((KVROWS, DH), jnp.int16),
+        in_specs=[ANY] * 4,
+        out_specs=VMEM,
+        scratch_shapes=[
+            pltpu.VMEM((4, 2 * TOK, DH), jnp.bfloat16),
+            pltpu.SemaphoreType.DMA((4,)),
+        ],
+        compiler_params=PARAMS,
+        name="code",
+    )(*map(flat, (seq_keys, seq_values, memory_keys, memory_values)))
     kv_all = lax.all_gather(kv, "seq", axis_index_groups=R_GROUPS)
-    q_all = lax.all_to_all(q_parts, "seq", 0, 0, axis_index_groups=C_GROUPS, tiled=True)
     parts = pl.pallas_call(
         attend_kernel,
         out_shape=jax.ShapeDtypeStruct((NC, OROWS, DH), jnp.bfloat16),
         in_specs=[SMEM, VMEM, VMEM],
         out_specs=VMEM,
+        scratch_shapes=[
+            pltpu.VMEM((4, NR * TOK, DH), jnp.bfloat16),
+            pltpu.VMEM((4, DH, NR * TOK), jnp.bfloat16),
+        ],
         compiler_params=PARAMS,
         name="attend",
     )(pos, q_all, kv_all)

time: 134 us -> 108 us (0.81)
  waiting for transfers between devices: 76.7 us -> 10.8 us
  blocking collectives: 11.7 us -> 68.9 us
  between operations: 14.1 us -> 0.73 us
  local copies, waits for them, and re-layouts: 6.51 us -> 1.58 us
  Pallas kernels: 13.3 us -> 15.3 us
    all_gather x1 -> x0, waiting for transfers between devices: 55.1 us -> none  [on_device(): kv_all = lax.all_gather(kv, 'seq', axis_index_groups=R_GROUPS)]
    all_gather x0 -> x1, blocking collectives: none -> 52.7 us  [on_device(): kv_all = lax.all_gather(kv, 'seq', axis_index_groups=R_GROUPS)]
    all_to_all x1, waiting for transfers between devices: 7.64 us -> 0.01 us  [on_device(): lax.all_to_all(q_parts, 'seq', 0, 0, axis_index_groups=C_GROUPS, tiled=True)]
    unnamed x18 -> x16, local copies, waits for them, and re-layouts: 6.44 us -> 1.51 us
    all_to_all x1, blocking collectives: 11.7 us -> 16.2 us  [on_device(): squares = lax.all_to_all(squares, 'head', 0, 0, tiled=True)]
    all_to_all x1, waiting for transfers between devices: 14 us -> 10.8 us  [on_device(): lax.all_to_all(parts, 'seq', 0, 0, axis_index_groups=C_GROUPS, tiled=True)]
    pallas_call x1 -> x2, Pallas kernels: 1.85 us -> 3.37 us  [the longest x1 1.8 us: on_device(): pl.pallas_call(code_kernel, out_shape=jax.ShapeDtypeStruct((KVROWS, DH),...]
  transfers between devices with their start and end apart: 3 -> 2, of which waited for: 3 -> 1; matrix products, arithmetic and copies ran while one was open for 0% -> 0% of each run, Pallas kernels for 0% -> 2%
where the time goes in v2:
time: 108 us
  blocking collectives  68.9 us (64%)
  Pallas kernels  15.3 us (14%)
  waiting for transfers between devices  10.8 us (10%)
  starting transfers between devices  10.6 us (10%)
  local copies, waits for them, and re-layouts  1.58 us (1%)
    all_gather x1, blocking collectives, on_device(): kv_all = lax.all_gather(kv, 'seq', axis_index_groups=R_GROUPS)  52.7 us
    all_to_all x1, blocking collectives, on_device(): squares = lax.all_to_all(squares, 'head', 0, 0, tiled=True)  16.2 us
    all_to_all x1, waiting for transfers between devices, on_device(): lax.all_to_all(parts, 'seq', 0, 0, axis_index_groups=C_GROUPS, tiled=True)  10.8 us
    pallas_call x1, Pallas kernels, on_device(): pl.pallas_call(attend_kernel, out_shape=jax.ShapeDtypeStruct((NC, OROWS,...  10.7 us
    all_to_all x1, starting transfers between devices, on_device(): lax.all_to_all(q_parts, 'seq', 0, 0, axis_index_groups=C_GROUPS, tiled=True)  6.21 us
    all_to_all x1, starting transfers between devices, on_device(): lax.all_to_all(parts, 'seq', 0, 0, axis_index_groups=C_GROUPS, tiled=True)  4.4 us
  transfers between devices with their start and end apart: 2, of which 1 were waited for; matrix products, arithmetic and copies ran while one was open for 0% of the time, Pallas kernels for 2%

profile of v2, /device:TPU:1, one launch (start us, length us, event | category | flops | bytes accessed | tf_op | source)
XLA Modules:
  0.0 108.0 jit_solution(9060441808798390781)
XLA Ops:
  0.7 0.0 copy-start
  0.7 0.8 copy-done
  1.5 0.0 copy-start.6
  1.5 0.7 copy-done.6
  2.2 1.6 %query.1 = bf16[8,272,128]{2,1,0:T(8,128)(2,1)} custom-call(s32[1,8]{1,0:T(1,128)S(1)} %copy-done.6, s32[1]{0:T(128)S(6)} %copy.11.fifo_hbm, bf16[256,128]{1,0:T(8,128)(2,1)S(1)} %bitcast.15), custom_call_target="tpu_custom_call" | custom-call | tf_op jit(solution)/shard_map/query/pallas_call | solution.py:208
  3.7 6.2 %all-to-all-start = ((bf16[8,272,128]{2,1,0:T(8,128)(2,1)}), bf16[8,272,128]{2,1,0:T(8,128)(2,1)S(1)}, u32[]{:S(2)}, u32[]{:S(2)}) async-start(bf16[8,272,128]{2,1,0:T(8,128)(2,1)} %query.1), calls=%async_computation | async-start | bytes 1114112 | tf_op jit(solution)/shard_map/all_to_all | solution.py:222
  9.9 0.0 copy-done.1
  10.0 0.0 copy-done.2
  10.0 0.0 copy-done.3
  10.0 0.0 copy-done.4
  10.0 1.8 %code.1 = s16[1040,128]{1,0:T(8,128)(2,1)S(1)} custom-call(bf16[256,128]{1,0:T(8,128)(2,1)S(1)} %bitcast.16, bf16[256,128]{1,0:T(8,128)(2,1)S(1)} %bitcast.17, bf16[256,128]{1,0:T(8,128)(2,1)S(1)} %bitcast.18, bf16[256,128]{1,0:T(8,128)(2,1)S(1)} %bitcast.19), custom_call_target="tpu_custom_call" | custom-call | tf_op jit(solution)/shard_map/code/pallas_call | solution.py:223
  11.8 0.1 pad_add_fusion.pos_ref
  11.9 52.7 %all-gather.2 = s16[8320,128]{1,0:T(8,128)(2,1)S(1)} all-gather(s16[1040,128]{1,0:T(8,128)(2,1)S(1)} %code.1), channel_id=2, replica_groups={{0,16,32,48,64,80,96,112},{8,24,40,56,72,88,104,120},{128,144,160,176,1..., dimensions={0}, use_global_device_ids=true | all-gather | bytes 2396160 | tf_op jit(solution)/shard_map/all_gather | solution.py:235
  64.6 0.0 all-to-all-done.q_ref
  64.6 10.7 %attend.1 = bf16[8,528,128]{2,1,0:T(8,128)(2,1)} custom-call(s32[3]{0:T(128)S(1)} %pad_add_fusion.pos_ref, bf16[8,272,128]{2,1,0:T(8,128)(2,1)S(1)} %all-to-all-done.q_ref, s16[8,1040,128]{2,1,0:T(8,128)(2,1)S(1)} %bitcast.14), custom_call_target="tpu_custom_call" | custom-call | tf_op jit(solution)/shard_map/attend/pallas_call | solution.py:236
  75.3 4.4 %all-to-all-start.1 = ((bf16[8,528,128]{2,1,0:T(8,128)(2,1)}), bf16[8,528,128]{2,1,0:T(8,128)(2,1)S(1)}, u32[]{:S(2)}, u32[]{:S(2)}) async-start(bf16[8,528,128]{2,1,0:T(8,128)(2,1)} %attend.1), calls=%async_computation.1 | async-start | bytes 2162688 | tf_op jit(solution)/shard_map/all_to_all | solution.py:248
  79.7 0.0 copy-done.7
  79.7 0.0 copy-start.5
  79.7 10.8 %all-to-all-done.1.part_ref = bf16[8,528,128]{2,1,0:T(8,128)(2,1)S(1)} async-done(((bf16[8,528,128]{2,1,0:T(8,128)(2,1)}), bf16[8,528,128]{2,1,0:T(8,128)(2,1)S(1)}, u32[]{:S(2)}, u32[]{:S(2)}) %all-to-all-start.1) | async-done | bytes 1081376 | tf_op jit(solution)/shard_map/all_to_all | solution.py:248
  90.5 0.1 broadcast_in_dim.2.gate_ref
  90.6 0.3 merge.1
  90.9 16.2 %all_to_all.21 = f32[8,1,128]{2,1,0:T(1,128)S(1)} all-to-all(f32[8,1,128]{2,1,0:T(1,128)S(1)} %bitcast.21), channel_id=1, replica_groups=mesh['seq'=64,'head'=8] {'head'}, dimensions={0} | all-to-all | bytes 8192 | tf_op jit(solution)/shard_map/all_to_all | solution.py:261
  107.1 0.0 copy-done.5
  107.1 0.9 final.1
  (6 shorter events, 0.0 us)
Async XLA Ops:
  0.7 0.8 copy-start
  1.5 0.7 copy-start.6
  2.1 7.8 %copy-start.1 = (bf16[128,2,128]{2,1,0:T(2,128)(2,1)S(1)}, bf16[128,2,128]{2,1,0:T(2,128)(2,1)}, u32[]{:S(2)}) copy-start(bf16[128,2,128]{2,1,0:T(2,128)(2,1)} %param.10) | copy-start | bytes 196612
  2.2 7.8 %copy-start.2 = (bf16[128,2,128]{2,1,0:T(2,128)(2,1)S(1)}, bf16[128,2,128]{2,1,0:T(2,128)(2,1)}, u32[]{:S(2)}) copy-start(bf16[128,2,128]{2,1,0:T(2,128)(2,1)} %param.11) | copy-start | bytes 196612
  2.2 7.8 %copy-start.3 = (bf16[128,2,128]{2,1,0:T(2,128)(2,1)S(1)}, bf16[128,2,128]{2,1,0:T(2,128)(2,1)}, u32[]{:S(2)}) copy-start(bf16[128,2,128]{2,1,0:T(2,128)(2,1)} %param.12) | copy-start | bytes 196612
  2.2 7.8 %copy-start.4 = (bf16[128,2,128]{2,1,0:T(2,128)(2,1)S(1)}, bf16[128,2,128]{2,1,0:T(2,128)(2,1)}, u32[]{:S(2)}) copy-start(bf16[128,2,128]{2,1,0:T(2,128)(2,1)} %param.13) | copy-start | bytes 196612
  3.7 60.8 %all-to-all-start = ((bf16[8,272,128]{2,1,0:T(8,128)(2,1)}), bf16[8,272,128]{2,1,0:T(8,128)(2,1)S(1)}, u32[]{:S(2)}, u32[]{:S(2)}) async-start(bf16[8,272,128]{2,1,0:T(8,128)(2,1)} %query.1), calls=%async_computation | async-start | bytes 1114112 | tf_op jit(solution)/shard_map/all_to_all | solution.py:222
  75.3 4.4 %copy-start.7 = (f32[2]{0:T(128)S(1)}, f32[2]{0:T(128)}, u32[]{:S(2)}) copy-start(f32[2]{0:T(128)} %param.16) | copy-start | bytes 28
  75.3 15.2 %all-to-all-start.1 = ((bf16[8,528,128]{2,1,0:T(8,128)(2,1)}), bf16[8,528,128]{2,1,0:T(8,128)(2,1)S(1)}, u32[]{:S(2)}, u32[]{:S(2)}) async-start(bf16[8,528,128]{2,1,0:T(8,128)(2,1)} %attend.1), calls=%async_computation.1 | async-start | bytes 2162688 | tf_op jit(solution)/shard_map/all_to_all | solution.py:248
  79.7 27.4 %copy-start.5 = (f32[2,128]{1,0:T(2,128)S(1)}, f32[2,128]{1,0:T(2,128)}, u32[]{:S(2)}) copy-start(f32[2,128]{1,0:T(2,128)} %gain_ref.1) | copy-start | bytes 3076

commit v3 on v2

--- a/solution.py
+++ b/solution.py
@@ -87,15 +87,18 @@
     kv_out[pl.ds(8 * TOK, 16), :] = tile.astype(jnp.int16)
 
 
+def tok_start(r):
+    return r * TOK if isinstance(r, int) else pl.multiple_of(r * TOK, TOK)
+
+
 def decode(kv_ref, keys_ref, vals_ref):
     for r in range(NR):
         power = kv_ref[r, pl.ds(8 * TOK, 16), :].astype(jnp.int32).astype(jnp.float32)
         factor = jnp.exp2(-power)
         for i in range(4):
             for h in range(2):
-                code = kv_ref[r, pl.ds((i * 2 + h) * TOK, TOK), :].astype(jnp.int32)
-                block = code.astype(jnp.float32) * factor[i * 2 + h : i * 2 + h + 1, :]
-                block = block.astype(jnp.bfloat16)
+                code = kv_ref[r, pl.ds((i * 2 + h) * TOK, TOK), :].astype(jnp.bfloat16)
+                block = code * factor[i * 2 + h : i * 2 + h + 1, :].astype(jnp.bfloat16)
                 at = (i // 2) * 2 + h
                 if i % 2:
                     vals_ref[at, :, pl.ds(r * TOK, TOK)] = block
@@ -103,55 +106,107 @@
                     keys_ref[at, pl.ds(r * TOK, TOK), :] = block
 
 
-def attend_kernel(pos_ref, q_ref, kv_ref, out_ref, keys_ref, vals_ref):
+def attend_kernel(
+    pos_ref, q_ref, kv_ref, out_ref, keys_ref, vals_ref, s_ref, bias_ref, stat_ref, slot_ref
+):
     decode(kv_ref, keys_ref, vals_ref)
     my_x, my_pair, my_par = pos_ref[0], pos_ref[1], pos_ref[2]
     ahead = lax.broadcasted_iota(jnp.int32, (TOK, 2 * TOK), 0) - lax.broadcasted_iota(
         jnp.int32, (TOK, 2 * TOK), 1
     )
+    row = lax.broadcasted_iota(jnp.int32, (16, TOK), 0)
+    place = jnp.where(row < NR, jnp.left_shift(1, row), 0).astype(jnp.float32)
+
+    def run(xq, kind, blocks, mask):
+        tops = []
+        for h in range(2):
+            at = kind * 2 + h
+            q_rows = jnp.concatenate(
+                [q_ref[2 * xq + par, pl.ds(h * TOK, TOK), :] for par in range(2)], 0
+            )
+            top = jnp.full((8, 2 * TOK), FLOOR, jnp.float32)
+            for i, r in enumerate(blocks):
+                s = mask(i, dot(keys_ref[at, pl.ds(tok_start(r), TOK), :], q_rows, NT))
+                s_ref[at, pl.ds(i * TOK, TOK), :] = s
+                top = jnp.maximum(top, jnp.max(s.reshape(TOK // 8, 8, 2 * TOK), 0))
+            tops.append(jnp.max(top, 0, keepdims=True) * LOG2_SCALE)
+        for h in range(2):
+            at = kind * 2 + h
+            top = tops[h]
+            total = jnp.zeros((8, 2 * TOK), jnp.float32)
+            acc = jnp.zeros((DH, 2 * TOK), jnp.float32)
+            for i in range(0, len(blocks), 2):
+                e = jnp.exp2(s_ref[at, pl.ds(i * TOK, 2 * TOK), :] * LOG2_SCALE - top)
+                total = total + jnp.sum(e.reshape(2 * TOK // 8, 8, 2 * TOK), 0)
+                vals = jnp.concatenate(
+                    [vals_ref[at, :, pl.ds(tok_start(r), TOK)] for r in blocks[i : i + 2]], 1
+                )
+                acc = acc + dot(vals, e.astype(jnp.bfloat16), NN)
+            total = jnp.maximum(jnp.sum(total, 0, keepdims=True), 1e-30)
+            acc = (acc * (1.0 / total)).astype(jnp.bfloat16)
+            for par in range(2):
+                out_ref[2 * xq + par, pl.ds(at * DH, DH), :] = acc[:, par * TOK : (par + 1) * TOK]
+            lse = top + jnp.log2(total)
+            for i in range(3):
+                part = lse.astype(jnp.bfloat16).astype(jnp.float32)
+                stat_ref[at * 3 + i : at * 3 + i + 1, :] = part
+                lse = lse - part
 
     def step(xq, carry):
-        stats = []
+        def causal(r, s):
+            gap = ((xq - my_x) * NZ + 2 * my_pair - 2 * r - my_par) * TOK
+            return jnp.where(ahead <= gap, s, NEG)
+
         extra = [q_ref[2 * xq + par, pl.ds(2 * TOK, 16), :].astype(jnp.float32) for par in range(2)]
-        bias = jnp.concatenate(extra, 1)
-        for kind in range(2):
-            for h in range(2):
-                q_rows = jnp.concatenate(
-                    [q_ref[2 * xq + par, pl.ds(h * TOK, TOK), :] for par in range(2)], 0
-                )
-                scores = []
-                for r in range(NR):
-                    keys = keys_ref[kind * 2 + h, pl.ds(r * TOK, TOK), :]
-                    s = dot(keys, q_rows, NT)
-                    if kind == 0:
-                        gap = ((xq - my_x) * NZ + 2 * my_pair - 2 * r - my_par) * TOK
-                        s = jnp.where(ahead <= gap, s, NEG)
-                    else:
-                        s = s + bias[r : r + 1, :]
-                    scores.append(s)
-                s = jnp.concatenate(scores, 0)
-                top = jnp.maximum(jnp.max(s, 0, keepdims=True), FLOOR) * LOG2_SCALE
-                e = jnp.exp2(s * LOG2_SCALE - top)
-                total = jnp.sum(e, 0, keepdims=True)
-                total = jnp.maximum(total, 1e-30)
-                acc = dot(vals_ref[kind * 2 + h], e.astype(jnp.bfloat16), NN) * (1.0 / total)
-                acc = acc.astype(jnp.bfloat16)
-                for par in range(2):
-                    out_ref[2 * xq + par, pl.ds((kind * 2 + h) * DH, DH), :] = acc[
-                        :, par * TOK : (par + 1) * TOK
-                    ]
-                lse = top + jnp.log2(total)
-                for _ in range(3):
-                    part = lse.astype(jnp.bfloat16).astype(jnp.float32)
-                    stats.append(part)
-                    lse = lse - part
-        stats.append(jnp.zeros((4, 2 * TOK), jnp.float32))
-        tile = jnp.concatenate(stats, 0).astype(jnp.bfloat16)
+        bias_ref[...] = jnp.concatenate(extra, 1)
+        wanted = jnp.where(jnp.maximum(extra[0], extra[1]) > -1.0, place, 0.0)
+        bits = jnp.max(jnp.sum(wanted, 0, keepdims=True)).astype(jnp.int32)
+        for r in range(NR):
+            slot_ref[r] = 0
+        count = jnp.int32(0)
+        for r in range(NR):
+            slot_ref[count] = r
+            count = count + (jnp.right_shift(bits, r) & 1)
+
+        run(xq, 0, list(range(NR)), causal)
+
+        def some(size):
+            blocks = [slot_ref[i] for i in range(size)]
+
+            def retrieved(i, s):
+                return s + jnp.where(i < count, bias_ref[pl.ds(blocks[i], 1), :], NEG)
+
+            run(xq, 1, blocks, retrieved)
+
+        @pl.when(count <= 2)
+        def _():
+            some(2)
+
+        @pl.when((count > 2) & (count <= 4))
+        def _():
+            some(4)
+
+        @pl.when(count > 4)
+        def _():
+            some(8)
+
+        tile = stat_ref[...].astype(jnp.bfloat16)
         for par in range(2):
             out_ref[2 * xq + par, pl.ds(4 * DH, 16), :] = tile[:, par * TOK : (par + 1) * TOK]
         return carry
 
+    stat_ref[...] = jnp.zeros((16, 2 * TOK), jnp.float32)
     lax.fori_loop(0, NX, step, 0)
+
+
+SCRATCH = [
+    pltpu.VMEM((4, NR * TOK, DH), jnp.bfloat16),
+    pltpu.VMEM((4, DH, NR * TOK), jnp.bfloat16),
+    pltpu.VMEM((4, NR * TOK, 2 * TOK), jnp.float32),
+    pltpu.VMEM((16, 2 * TOK), jnp.float32),
+    pltpu.VMEM((16, 2 * TOK), jnp.float32),
+    pltpu.SMEM((8,), jnp.int32),
+]
 
 
 def merge_kernel(gate_ref, part_ref, comb_ref, sq_ref):
@@ -198,6 +253,7 @@
 VMEM = pl.BlockSpec(memory_space=pltpu.VMEM)
 ANY = pl.BlockSpec(memory_space=pl.ANY)
 SMEM = pl.BlockSpec(memory_space=pltpu.SMEM)
+WHOLE = pltpu.CompilerParams(vmem_limit_bytes=63 * 2**20)
 PARAMS = pltpu.CompilerParams(vmem_limit_bytes=40 * 2**20)
 
 
@@ -216,7 +272,7 @@
             pltpu.VMEM((2 * TOK, DH), jnp.bfloat16),
             pltpu.SemaphoreType.DMA((3,)),
         ],
-        compiler_params=PARAMS,
+        compiler_params=WHOLE,
         name="query",
     )(retrieval, fifo_head, flat(queries))
     q_all = lax.all_to_all(q_parts, "seq", 0, 0, axis_index_groups=C_GROUPS, tiled=True)
@@ -229,7 +285,7 @@
             pltpu.VMEM((4, 2 * TOK, DH), jnp.bfloat16),
             pltpu.SemaphoreType.DMA((4,)),
         ],
-        compiler_params=PARAMS,
+        compiler_params=WHOLE,
         name="code",
     )(*map(flat, (seq_keys, seq_values, memory_keys, memory_values)))
     kv_all = lax.all_gather(kv, "seq", axis_index_groups=R_GROUPS)
@@ -238,10 +294,7 @@
         out_shape=jax.ShapeDtypeStruct((NC, OROWS, DH), jnp.bfloat16),
         in_specs=[SMEM, VMEM, VMEM],
         out_specs=VMEM,
-        scratch_shapes=[
-            pltpu.VMEM((4, NR * TOK, DH), jnp.bfloat16),
-            pltpu.VMEM((4, DH, NR * TOK), jnp.bfloat16),
-        ],
+        scratch_shapes=SCRATCH,
         compiler_params=PARAMS,
         name="attend",
     )(pos, q_all, kv_all)

time: 108 us -> 104 us (0.963)
  blocking collectives: 68.9 us -> 64.9 us
  starting transfers between devices: 10.6 us -> 12.5 us
  local copies, waits for them, and re-layouts: 1.58 us -> 0.08 us
    all_gather x1, blocking collectives: 52.7 us -> 49.3 us  [on_device(): kv_all = lax.all_gather(kv, 'seq', axis_index_groups=R_GROUPS)]
    all_to_all x1, starting transfers between devices: 4.4 us -> 6.32 us  [on_device(): lax.all_to_all(parts, 'seq', 0, 0, axis_index_groups=C_GROUPS, tiled=True)]
    pallas_call x1, Pallas kernels: 10.7 us -> 8.82 us  [on_device(): pl.pallas_call(attend_kernel, out_shape=jax.ShapeDtypeStruct((NC, OROWS,...]
    unnamed x16 -> x4, local copies, waits for them, and re-layouts: 1.51 us -> 0.01 us
    pallas_call x1, Pallas kernels: 1.8 us -> 2.97 us  [on_device(): pl.pallas_call(code_kernel, out_shape=jax.ShapeDtypeStruct((KVROWS, DH),...]
  transfers between devices with their start and end apart: 2 -> 2, of which waited for: 1 -> 1; matrix products, arithmetic and copies ran while one was open for 0% -> 0% of each run, Pallas kernels for 2% -> 3%
where the time goes in v3:
time: 104 us
  blocking collectives  64.9 us (62%)
  Pallas kernels  14.8 us (14%)
  starting transfers between devices  12.5 us (12%)
  waiting for transfers between devices  10.6 us (10%)
    all_gather x1, blocking collectives, on_device(): kv_all = lax.all_gather(kv, 'seq', axis_index_groups=R_GROUPS)  49.3 us
    all_to_all x1, blocking collectives, on_device(): squares = lax.all_to_all(squares, 'head', 0, 0, tiled=True)  15.6 us
    all_to_all x1, waiting for transfers between devices, on_device(): lax.all_to_all(parts, 'seq', 0, 0, axis_index_groups=C_GROUPS, tiled=True)  10.6 us
    pallas_call x1, Pallas kernels, on_device(): pl.pallas_call(attend_kernel, out_shape=jax.ShapeDtypeStruct((NC, OROWS,...  8.82 us
    all_to_all x1, starting transfers between devices, on_device(): lax.all_to_all(parts, 'seq', 0, 0, axis_index_groups=C_GROUPS, tiled=True)  6.32 us
    all_to_all x1, starting transfers between devices, on_device(): lax.all_to_all(q_parts, 'seq', 0, 0, axis_index_groups=C_GROUPS, tiled=True)  6.22 us
    pallas_call x1, Pallas kernels, on_device(): pl.pallas_call(code_kernel, out_shape=jax.ShapeDtypeStruct((KVROWS, DH),...  2.97 us
  transfers between devices with their start and end apart: 2, of which 1 were waited for; matrix products, arithmetic and copies ran while one was open for 0% of the time, Pallas kernels for 3%

profile of v3, /device:TPU:1, one launch (start us, length us, event | category | flops | bytes accessed | tf_op | source)
XLA Modules:
  0.0 103.8 jit_solution(15997881051059305869)
XLA Ops:
  0.7 1.9 %query.1 = bf16[8,272,128]{2,1,0:T(8,128)(2,1)} custom-call(s32[1,8]{1,0:T(1,128)} %want_hbm.1, s32[1]{0:T(128)S(6)} %copy.11.fifo_hbm, bf16[256,128]{1,0:T(8,128)(2,1)} %bitcast.17), custom_call_target="tpu_custom_call" | custom-call | tf_op jit(solution)/shard_map/query/pallas_call | solution.py:264
  2.5 6.2 %all-to-all-start = ((bf16[8,272,128]{2,1,0:T(8,128)(2,1)}), bf16[8,272,128]{2,1,0:T(8,128)(2,1)S(1)}, u32[]{:S(2)}, u32[]{:S(2)}) async-start(bf16[8,272,128]{2,1,0:T(8,128)(2,1)} %query.1), calls=%async_computation | async-start | bytes 1114112 | tf_op jit(solution)/shard_map/all_to_all | solution.py:278
  8.7 3.0 %code.1 = s16[1040,128]{1,0:T(8,128)(2,1)} custom-call(bf16[256,128]{1,0:T(8,128)(2,1)} %bitcast.18, bf16[256,128]{1,0:T(8,128)(2,1)} %bitcast.19, bf16[256,128]{1,0:T(8,128)(2,1)} %bitcast.20, bf16[256,128]{1,0:T(8,128)(2,1)} %bitcast.21), custom_call_target="tpu_custom_call" | custom-call | tf_op jit(solution)/shard_map/code/pallas_call | solution.py:279
  11.7 0.1 pad_add_fusion.pos_ref
  11.8 49.3 %all-gather.2 = s16[8320,128]{1,0:T(8,128)(2,1)S(1)} all-gather(s16[1040,128]{1,0:T(8,128)(2,1)} %code.1), channel_id=2, replica_groups={{0,16,32,48,64,80,96,112},{8,24,40,56,72,88,104,120},{128,144,160,176,1..., dimensions={0}, use_global_device_ids=true | all-gather | bytes 2396160 | tf_op jit(solution)/shard_map/all_gather | solution.py:291
  61.1 0.0 all-to-all-done.q_ref
  61.1 8.8 %attend.1 = bf16[8,528,128]{2,1,0:T(8,128)(2,1)} custom-call(s32[3]{0:T(128)S(1)} %pad_add_fusion.pos_ref, bf16[8,272,128]{2,1,0:T(8,128)(2,1)S(1)} %all-to-all-done.q_ref, s16[8,1040,128]{2,1,0:T(8,128)(2,1)S(1)} %bitcast.14), custom_call_target="tpu_custom_call" | custom-call | tf_op jit(solution)/shard_map/attend/pallas_call | solution.py:292
  70.0 0.0 copy-start.1
  70.0 6.3 %all-to-all-start.1 = ((bf16[8,528,128]{2,1,0:T(8,128)(2,1)}), bf16[8,528,128]{2,1,0:T(8,128)(2,1)S(1)}, u32[]{:S(2)}, u32[]{:S(2)}) async-start(bf16[8,528,128]{2,1,0:T(8,128)(2,1)} %attend.1), calls=%async_computation.1 | async-start | bytes 2162688 | tf_op jit(solution)/shard_map/all_to_all | solution.py:301
  76.3 0.0 copy-done.1
  76.3 0.0 copy-start
  76.3 10.6 %all-to-all-done.1.part_ref = bf16[8,528,128]{2,1,0:T(8,128)(2,1)S(1)} async-done(((bf16[8,528,128]{2,1,0:T(8,128)(2,1)}), bf16[8,528,128]{2,1,0:T(8,128)(2,1)S(1)}, u32[]{:S(2)}, u32[]{:S(2)}) %all-to-all-start.1) | async-done | bytes 1081376 | tf_op jit(solution)/shard_map/all_to_all | solution.py:301
  86.9 0.1 broadcast_in_dim.2.gate_ref
  87.0 0.3 merge.1
  87.3 15.6 %all_to_all.21 = f32[8,1,128]{2,1,0:T(1,128)S(1)} all-to-all(f32[8,1,128]{2,1,0:T(1,128)S(1)} %bitcast.16), channel_id=1, replica_groups=mesh['seq'=64,'head'=8] {'head'}, dimensions={0} | all-to-all | bytes 8192 | tf_op jit(solution)/shard_map/all_to_all | solution.py:314
  102.9 0.0 copy-done
  102.9 0.9 final.1
  (1 shorter events, 0.0 us)
Async XLA Ops:
  2.5 58.6 %all-to-all-start = ((bf16[8,272,128]{2,1,0:T(8,128)(2,1)}), bf16[8,272,128]{2,1,0:T(8,128)(2,1)S(1)}, u32[]{:S(2)}, u32[]{:S(2)}) async-start(bf16[8,272,128]{2,1,0:T(8,128)(2,1)} %query.1), calls=%async_computation | async-start | bytes 1114112 | tf_op jit(solution)/shard_map/all_to_all | solution.py:278
  70.0 6.3 %copy-start.1 = (f32[2]{0:T(128)S(1)}, f32[2]{0:T(128)}, u32[]{:S(2)}) copy-start(f32[2]{0:T(128)} %param.16) | copy-start | bytes 28
  70.0 17.0 %all-to-all-start.1 = ((bf16[8,528,128]{2,1,0:T(8,128)(2,1)}), bf16[8,528,128]{2,1,0:T(8,128)(2,1)S(1)}, u32[]{:S(2)}, u32[]{:S(2)}) async-start(bf16[8,528,128]{2,1,0:T(8,128)(2,1)} %attend.1), calls=%async_computation.1 | async-start | bytes 2162688 | tf_op jit(solution)/shard_map/all_to_all | solution.py:301
  76.3 26.6 %copy-start = (f32[2,128]{1,0:T(2,128)S(1)}, f32[2,128]{1,0:T(2,128)}, u32[]{:S(2)}) copy-start(f32[2,128]{1,0:T(2,128)} %gain_ref.1) | copy-start | bytes 3076

commit v4 on v3

--- a/solution.py
+++ b/solution.py
@@ -21,7 +21,12 @@
 LOG2_SCALE = DH**-0.5 * 1.4426950408889634
 
 R_GROUPS = [[x * NZ + 2 * r + par for r in range(NR)] for x in range(NX) for par in range(2)]
-C_GROUPS = [[x * NZ + 2 * k + par for x in range(NX) for par in range(2)] for k in range(NZ // 2)]
+NH = 8
+C_GROUPS = [
+    [(x * NZ + (2 * k + par + head % 2) % NZ) * NH + head for x in range(NX) for par in range(2)]
+    for head in range(NH)
+    for k in range(NZ // 2)
+]
 
 NT = (((1,), (1,)), ((), ()))
 NN = (((1,), (0,)), ((), ()))
@@ -39,6 +44,7 @@
 
 
 def query_kernel(want_hbm, fifo_hbm, q_hbm, q_out, want, fifo, q_in, sems):
+    core = lax.axis_index("head") % 2
     copies = [
         pltpu.make_async_copy(src, dst, sems.at[i])
         for i, (src, dst) in enumerate(((want_hbm, want), (fifo_hbm, fifo), (q_hbm, q_in)))
@@ -52,7 +58,7 @@
     row = lax.broadcasted_iota(jnp.int32, (16, TOK), 0)
     for c in range(NC):
         q_out[c, pl.ds(0, 2 * TOK), :] = q_rows
-        block = (c // 2) * NZ + 2 * row + c % 2
+        block = (c // 2) * NZ + 2 * row + (c + core) % 2
         chosen = block == want[0, 0]
         for i in range(1, 8):
             chosen = chosen | (block == want[0, i])
@@ -110,10 +116,10 @@
     pos_ref, q_ref, kv_ref, out_ref, keys_ref, vals_ref, s_ref, bias_ref, stat_ref, slot_ref
 ):
     decode(kv_ref, keys_ref, vals_ref)
-    my_x, my_pair, my_par = pos_ref[0], pos_ref[1], pos_ref[2]
-    ahead = lax.broadcasted_iota(jnp.int32, (TOK, 2 * TOK), 0) - lax.broadcasted_iota(
-        jnp.int32, (TOK, 2 * TOK), 1
-    )
+    my_x, my_par, first_z = pos_ref[0], pos_ref[1], pos_ref[2]
+    lane = lax.broadcasted_iota(jnp.int32, (TOK, 2 * TOK), 1)
+    ahead = lax.broadcasted_iota(jnp.int32, (TOK, 2 * TOK), 0) - lane
+    ahead = ahead + jnp.where((lane >= TOK) & (first_z == NZ - 1), NZ * TOK, 0)
     row = lax.broadcasted_iota(jnp.int32, (16, TOK), 0)
     place = jnp.where(row < NR, jnp.left_shift(1, row), 0).astype(jnp.float32)
 
@@ -154,7 +160,7 @@
 
     def step(xq, carry):
         def causal(r, s):
-            gap = ((xq - my_x) * NZ + 2 * my_pair - 2 * r - my_par) * TOK
+            gap = ((xq - my_x) * NZ + first_z - 2 * r - my_par) * TOK
             return jnp.where(ahead <= gap, s, NEG)
 
         extra = [q_ref[2 * xq + par, pl.ds(2 * TOK, 16), :].astype(jnp.float32) for par in range(2)]
@@ -259,7 +265,9 @@
 
 def on_device(queries, seq_keys, seq_values, memory_keys, memory_values, retrieval, fifo_head, head_gate, norm_gain):
     me = lax.axis_index("seq")
-    pos = jnp.stack([me // NZ, (me % NZ) // 2, me % 2]).astype(jnp.int32)
+    core = lax.axis_index("head") % 2
+    first_z = (me - core + NZ) % NZ // 2 * 2 + core
+    pos = jnp.stack([me // NZ, me % 2, first_z]).astype(jnp.int32)
     flat = lambda a: a.reshape(2 * TOK, DH)
     q_parts = pl.pallas_call(
         query_kernel,
@@ -275,7 +283,7 @@
         compiler_params=WHOLE,
         name="query",
     )(retrieval, fifo_head, flat(queries))
-    q_all = lax.all_to_all(q_parts, "seq", 0, 0, axis_index_groups=C_GROUPS, tiled=True)
+    q_all = lax.all_to_all(q_parts, ("seq", "head"), 0, 0, axis_index_groups=C_GROUPS, tiled=True)
     kv = pl.pallas_call(
         code_kernel,
         out_shape=jax.ShapeDtypeStruct((KVROWS, DH), jnp.int16),
@@ -285,7 +293,7 @@
             pltpu.VMEM((4, 2 * TOK, DH), jnp.bfloat16),
             pltpu.SemaphoreType.DMA((4,)),
         ],
-        compiler_params=WHOLE,
+        compiler_params=PARAMS,
         name="code",
     )(*map(flat, (seq_keys, seq_values, memory_keys, memory_values)))
     kv_all = lax.all_gather(kv, "seq", axis_index_groups=R_GROUPS)
@@ -298,7 +306,7 @@
         compiler_params=PARAMS,
         name="attend",
     )(pos, q_all, kv_all)
-    parts = lax.all_to_all(parts, "seq", 0, 0, axis_index_groups=C_GROUPS, tiled=True)
+    parts = lax.all_to_all(parts, ("seq", "head"), 0, 0, axis_index_groups=C_GROUPS, tiled=True)
     gate = jnp.broadcast_to(jax.nn.sigmoid(head_gate)[:, None], (2, TOK))
     comb, squares = pl.pallas_call(
         merge_kernel,

time: 104 us -> 106 us (1.019)
  blocking collectives: 64.9 us -> 51.7 us
  starting transfers between devices: 12.5 us -> 23.6 us
  waiting for transfers between devices: 10.6 us -> 15.6 us
  Pallas kernels: 14.8 us -> 13.5 us
    all_to_all x2, starting transfers between devices: 12.5 us -> 23.6 us  [the longest x1 14.1 us: on_device(): lax.all_to_all(q_parts, ('seq', 'head'), 0, 0, axis_index_groups=C_GROUPS...]
    all_to_all x1, blocking collectives: 15.6 us -> 8.31 us  [on_device(): squares = lax.all_to_all(squares, 'head', 0, 0, tiled=True)]
    all_gather x1, blocking collectives: 49.3 us -> 43.4 us  [on_device(): kv_all = lax.all_gather(kv, 'seq', axis_index_groups=R_GROUPS)]
    all_to_all x2, waiting for transfers between devices: 10.6 us -> 15.6 us  [the longest x1 15.6 us: on_device(): lax.all_to_all(parts, ('seq', 'head'), 0, 0, axis_index_groups=C_GROUPS,...]
    pallas_call x1, Pallas kernels: 2.97 us -> 1.81 us  [on_device(): pl.pallas_call(code_kernel, out_shape=jax.ShapeDtypeStruct((KVROWS, DH),...]
  transfers between devices with their start and end apart: 2 -> 2, of which waited for: 1 -> 1; matrix products, arithmetic and copies ran while one was open for 0% -> 0% of each run, Pallas kernels for 3% -> 2%
where the time goes in v4:
time: 106 us; the launch traced here: 105 us
  blocking collectives  51.7 us (49%)
  starting transfers between devices  23.6 us (22%)
  waiting for transfers between devices  15.6 us (15%)
  Pallas kernels  13.5 us (13%)
    all_gather x1, blocking collectives, on_device(): kv_all = lax.all_gather(kv, 'seq', axis_index_groups=R_GROUPS)  43.4 us
    all_to_all x1, waiting for transfers between devices, on_device(): lax.all_to_all(parts, ('seq', 'head'), 0, 0, axis_index_groups=C_GROUPS,...  15.6 us
    all_to_all x1, starting transfers between devices, on_device(): lax.all_to_all(q_parts, ('seq', 'head'), 0, 0, axis_index_groups=C_GROUPS...  14.1 us
    all_to_all x1, starting transfers between devices, on_device(): lax.all_to_all(parts, ('seq', 'head'), 0, 0, axis_index_groups=C_GROUPS,...  9.53 us
    pallas_call x1, Pallas kernels, on_device(): pl.pallas_call(attend_kernel, out_shape=jax.ShapeDtypeStruct((NC, OROWS,...  8.66 us
    all_to_all x1, blocking collectives, on_device(): squares = lax.all_to_all(squares, 'head', 0, 0, tiled=True)  8.31 us
  transfers between devices with their start and end apart: 2, of which 1 were waited for; matrix products, arithmetic and copies ran while one was open for 0% of the time, Pallas kernels for 2%

profile of v4, /device:TPU:1, one launch (start us, length us, event | category | flops | bytes accessed | tf_op | source)
XLA Modules:
  0.0 105.3 jit_solution(15300252326686168290)
XLA Ops:
  0.0 0.0 copy-start
  0.0 0.0 copy-start.1
  0.0 0.0 copy-start.3
  0.7 1.9 %query.1 = bf16[8,272,128]{2,1,0:T(8,128)(2,1)} custom-call(s32[1,8]{1,0:T(1,128)} %want_hbm.1, s32[1]{0:T(128)S(6)} %copy.11.fifo_hbm, bf16[256,128]{1,0:T(8,128)(2,1)} %bitcast.21), custom_call_target="tpu_custom_call" | custom-call | tf_op jit(solution)/shard_map/query/pallas_call | solution.py:272
  2.6 14.1 %all-to-all-start = ((bf16[8,272,128]{2,1,0:T(8,128)(2,1)}), bf16[8,272,128]{2,1,0:T(8,128)(2,1)S(1)}, u32[]{:S(2)}, u32[]{:S(2)}) async-start(bf16[8,272,128]{2,1,0:T(8,128)(2,1)} %query.1), calls=%async_computation | async-start | bytes 1114112 | tf_op jit(solution)/shard_map/all_to_all | solution.py:286
  16.7 0.0 copy-done
  16.7 0.0 copy-done.1
  16.7 0.0 copy-done.2
  16.7 0.0 copy-done.3
  16.7 1.8 %code.1 = s16[1040,128]{1,0:T(8,128)(2,1)S(1)} custom-call(bf16[256,128]{1,0:T(8,128)(2,1)S(1)} %bitcast.15, bf16[256,128]{1,0:T(8,128)(2,1)S(1)} %bitcast.16, bf16[256,128]{1,0:T(8,128)(2,1)S(1)} %bitcast.17, bf16[256,128]{1,0:T(8,128)(2,1)S(1)} %bitcast.18), custom_call_target="tpu_custom_call" | custom-call | tf_op jit(solution)/shard_map/code/pallas_call | solution.py:287
  18.5 0.1 pad_add_fusion.pos_ref
  18.6 43.4 %all-gather.2 = s16[8320,128]{1,0:T(8,128)(2,1)S(1)} all-gather(s16[1040,128]{1,0:T(8,128)(2,1)S(1)} %code.1), channel_id=2, replica_groups={{0,16,32,48,64,80,96,112},{8,24,40,56,72,88,104,120},{128,144,160,176,1..., dimensions={0}, use_global_device_ids=true | all-gather | bytes 2396160 | tf_op jit(solution)/shard_map/all_gather | solution.py:299
  61.9 0.0 all-to-all-done.q_ref
  61.9 8.7 %attend.1 = bf16[8,528,128]{2,1,0:T(8,128)(2,1)} custom-call(s32[3]{0:T(128)S(1)} %pad_add_fusion.pos_ref, bf16[8,272,128]{2,1,0:T(8,128)(2,1)S(1)} %all-to-all-done.q_ref, s16[8,1040,128]{2,1,0:T(8,128)(2,1)S(1)} %bitcast.14), custom_call_target="tpu_custom_call" | custom-call | tf_op jit(solution)/shard_map/attend/pallas_call | solution.py:300
  70.6 0.0 copy-start.5
  70.6 9.5 %all-to-all-start.1 = ((bf16[8,528,128]{2,1,0:T(8,128)(2,1)}), bf16[8,528,128]{2,1,0:T(8,128)(2,1)S(1)}, u32[]{:S(2)}, u32[]{:S(2)}) async-start(bf16[8,528,128]{2,1,0:T(8,128)(2,1)} %attend.1), calls=%async_computation.1 | async-start | bytes 2162688 | tf_op jit(solution)/shard_map/all_to_all | solution.py:309
  80.1 0.0 copy-done.5
  80.1 0.0 copy-start.4
  80.1 15.6 %all-to-all-done.1.part_ref = bf16[8,528,128]{2,1,0:T(8,128)(2,1)S(1)} async-done(((bf16[8,528,128]{2,1,0:T(8,128)(2,1)}), bf16[8,528,128]{2,1,0:T(8,128)(2,1)S(1)}, u32[]{:S(2)}, u32[]{:S(2)}) %all-to-all-start.1) | async-done | bytes 1081376 | tf_op jit(solution)/shard_map/all_to_all | solution.py:309
  95.8 0.1 broadcast_in_dim.2.gate_ref
  95.8 0.3 merge.1
  96.1 8.3 %all_to_all.21 = f32[8,1,128]{2,1,0:T(1,128)S(1)} all-to-all(f32[8,1,128]{2,1,0:T(1,128)S(1)} %bitcast.20), channel_id=1, replica_groups=mesh['seq'=64,'head'=8] {'head'}, dimensions={0} | all-to-all | bytes 8192 | tf_op jit(solution)/shard_map/all_to_all | solution.py:322
  104.4 0.0 copy-done.4
  104.4 0.9 final.1
  (2 shorter events, 0.0 us)
Async XLA Ops:
  0.0 16.7 %copy-start = (bf16[128,2,128]{2,1,0:T(2,128)(2,1)S(1)}, bf16[128,2,128]{2,1,0:T(2,128)(2,1)}, u32[]{:S(2)}) copy-start(bf16[128,2,128]{2,1,0:T(2,128)(2,1)} %param.10) | copy-start | bytes 196612
  0.0 16.7 %copy-start.1 = (bf16[128,2,128]{2,1,0:T(2,128)(2,1)S(1)}, bf16[128,2,128]{2,1,0:T(2,128)(2,1)}, u32[]{:S(2)}) copy-start(bf16[128,2,128]{2,1,0:T(2,128)(2,1)} %param.11) | copy-start | bytes 196612
  0.0 16.7 %copy-start.2 = (bf16[128,2,128]{2,1,0:T(2,128)(2,1)S(1)}, bf16[128,2,128]{2,1,0:T(2,128)(2,1)}, u32[]{:S(2)}) copy-start(bf16[128,2,128]{2,1,0:T(2,128)(2,1)} %param.12) | copy-start | bytes 196612
  0.0 16.7 %copy-start.3 = (bf16[128,2,128]{2,1,0:T(2,128)(2,1)S(1)}, bf16[128,2,128]{2,1,0:T(2,128)(2,1)}, u32[]{:S(2)}) copy-start(bf16[128,2,128]{2,1,0:T(2,128)(2,1)} %param.13) | copy-start | bytes 196612
  2.6 59.4 %all-to-all-start = ((bf16[8,272,128]{2,1,0:T(8,128)(2,1)}), bf16[8,272,128]{2,1,0:T(8,128)(2,1)S(1)}, u32[]{:S(2)}, u32[]{:S(2)}) async-start(bf16[8,272,128]{2,1,0:T(8,128)(2,1)} %query.1), calls=%async_computation | async-start | bytes 1114112 | tf_op jit(solution)/shard_map/all_to_all | solution.py:286
  70.6 9.5 %copy-start.5 = (f32[2]{0:T(128)S(1)}, f32[2]{0:T(128)}, u32[]{:S(2)}) copy-start(f32[2]{0:T(128)} %param.16) | copy-start | bytes 28
  70.6 25.2 %all-to-all-start.1 = ((bf16[8,528,128]{2,1,0:T(8,128)(2,1)}), bf16[8,528,128]{2,1,0:T(8,128)(2,1)S(1)}, u32[]{:S(2)}, u32[]{:S(2)}) async-start(bf16[8,528,128]{2,1,0:T(8,128)(2,1)} %attend.1), calls=%async_computation.1 | async-start | bytes 2162688 | tf_op jit(solution)/shard_map/all_to_all | solution.py:309
  80.1 24.3 %copy-start.4 = (f32[2,128]{1,0:T(2,128)S(1)}, f32[2,128]{1,0:T(2,128)}, u32[]{:S(2)}) copy-start(f32[2,128]{1,0:T(2,128)} %gain_ref.1) | copy-start | bytes 3076

commit v5 on v3

--- a/solution.py
+++ b/solution.py
@@ -46,18 +46,20 @@
     for copy in copies:
         copy.start()
     perm = split_perm()
-    for copy in copies:
-        copy.wait()
-    q_rows = dot(perm, q_in[...], NN).astype(jnp.bfloat16)
     row = lax.broadcasted_iota(jnp.int32, (16, TOK), 0)
+    copies[0].wait()
+    copies[1].wait()
     for c in range(NC):
-        q_out[c, pl.ds(0, 2 * TOK), :] = q_rows
         block = (c // 2) * NZ + 2 * row + c % 2
         chosen = block == want[0, 0]
         for i in range(1, 8):
             chosen = chosen | (block == want[0, i])
         live = ((block - fifo[0] + BLOCKS) & (BLOCKS - 1)) >= EXPIRED
         q_out[c, pl.ds(2 * TOK, 16), :] = jnp.where(chosen & live, 0.0, NEG).astype(jnp.bfloat16)
+    copies[2].wait()
+    q_rows = dot(perm, q_in[...], NN).astype(jnp.bfloat16)
+    for c in range(NC):
+        q_out[c, pl.ds(0, 2 * TOK), :] = q_rows
 
 
 def code_kernel(k_hbm, v_hbm, mk_hbm, mv_hbm, kv_out, rows_in, sems):
@@ -101,7 +103,7 @@
                 block = code * factor[i * 2 + h : i * 2 + h + 1, :].astype(jnp.bfloat16)
                 at = (i // 2) * 2 + h
                 if i % 2:
-                    vals_ref[at, :, pl.ds(r * TOK, TOK)] = block
+                    vals_ref[at, pl.ds(0, DH), pl.ds(r * TOK, TOK)] = block
                 else:
                     keys_ref[at, pl.ds(r * TOK, TOK), :] = block
 
@@ -110,6 +112,8 @@
     pos_ref, q_ref, kv_ref, out_ref, keys_ref, vals_ref, s_ref, bias_ref, stat_ref, slot_ref
 ):
     decode(kv_ref, keys_ref, vals_ref)
+    for at in range(4):
+        vals_ref[at, pl.ds(DH, 16), :] = jnp.ones((16, NR * TOK), jnp.bfloat16)
     my_x, my_pair, my_par = pos_ref[0], pos_ref[1], pos_ref[2]
     ahead = lax.broadcasted_iota(jnp.int32, (TOK, 2 * TOK), 0) - lax.broadcasted_iota(
         jnp.int32, (TOK, 2 * TOK), 1
@@ -133,17 +137,14 @@
         for h in range(2):
             at = kind * 2 + h
             top = tops[h]
-            total = jnp.zeros((8, 2 * TOK), jnp.float32)
-            acc = jnp.zeros((DH, 2 * TOK), jnp.float32)
+            acc = jnp.zeros((DH + 16, 2 * TOK), jnp.float32)
             for i in range(0, len(blocks), 2):
-                e = jnp.exp2(s_ref[at, pl.ds(i * TOK, 2 * TOK), :] * LOG2_SCALE - top)
-                total = total + jnp.sum(e.reshape(2 * TOK // 8, 8, 2 * TOK), 0)
-                vals = jnp.concatenate(
-                    [vals_ref[at, :, pl.ds(tok_start(r), TOK)] for r in blocks[i : i + 2]], 1
-                )
+                part = blocks[i : i + 2]
+                e = jnp.exp2(s_ref[at, pl.ds(i * TOK, len(part) * TOK), :] * LOG2_SCALE - top)
+                vals = jnp.concatenate([vals_ref[at, :, pl.ds(tok_start(r), TOK)] for r in part], 1)
                 acc = acc + dot(vals, e.astype(jnp.bfloat16), NN)
-            total = jnp.maximum(jnp.sum(total, 0, keepdims=True), 1e-30)
-            acc = (acc * (1.0 / total)).astype(jnp.bfloat16)
+            total = jnp.maximum(acc[DH : DH + 1, :], 1e-30)
+            acc = (acc[:DH, :] * (1.0 / total)).astype(jnp.bfloat16)
             for par in range(2):
                 out_ref[2 * xq + par, pl.ds(at * DH, DH), :] = acc[:, par * TOK : (par + 1) * TOK]
             lse = top + jnp.log2(total)
@@ -201,7 +202,7 @@
 
 SCRATCH = [
     pltpu.VMEM((4, NR * TOK, DH), jnp.bfloat16),
-    pltpu.VMEM((4, DH, NR * TOK), jnp.bfloat16),
+    pltpu.VMEM((4, DH + 16, NR * TOK), jnp.bfloat16),
     pltpu.VMEM((4, NR * TOK, 2 * TOK), jnp.float32),
     pltpu.VMEM((16, 2 * TOK), jnp.float32),
     pltpu.VMEM((16, 2 * TOK), jnp.float32),
@@ -285,7 +286,7 @@
             pltpu.VMEM((4, 2 * TOK, DH), jnp.bfloat16),
             pltpu.SemaphoreType.DMA((4,)),
         ],
-        compiler_params=WHOLE,
+        compiler_params=PARAMS,
         name="code",
     )(*map(flat, (seq_keys, seq_values, memory_keys, memory_values)))
     kv_all = lax.all_gather(kv, "seq", axis_index_groups=R_GROUPS)

time: 104 us -> 103 us (level)
  Pallas kernels: 14.8 us -> 13 us
  starting transfers between devices: 12.5 us -> 10.9 us
  waiting for transfers between devices: 10.6 us -> 11.9 us
  blocking collectives: 64.9 us -> 66.1 us
    all_gather x1, blocking collectives: 49.3 us -> 52.7 us  [on_device(): kv_all = lax.all_gather(kv, 'seq', axis_index_groups=R_GROUPS)]
    all_to_all x1, blocking collectives: 15.6 us -> 13.4 us  [on_device(): squares = lax.all_to_all(squares, 'head', 0, 0, tiled=True)]
    all_to_all x1, starting transfers between devices: 6.32 us -> 4.68 us  [on_device(): lax.all_to_all(parts, 'seq', 0, 0, axis_index_groups=C_GROUPS, tiled=True)]
    all_to_all x1, waiting for transfers between devices: 10.6 us -> 11.9 us  [on_device(): lax.all_to_all(parts, 'seq', 0, 0, axis_index_groups=C_GROUPS, tiled=True)]
    pallas_call x1, Pallas kernels: 2.97 us -> 1.81 us  [on_device(): pl.pallas_call(code_kernel, out_shape=jax.ShapeDtypeStruct((KVROWS, DH),...]
  transfers between devices with their start and end apart: 2 -> 2, of which waited for: 1 -> 1; matrix products, arithmetic and copies ran while one was open for 0% -> 0% of each run, Pallas kernels for 3% -> 2%
where the time goes in v5:
time: 103 us
  blocking collectives  66.1 us (64%)
  Pallas kernels  13 us (13%)
  waiting for transfers between devices  11.9 us (12%)
  starting transfers between devices  10.9 us (11%)
    all_gather x1, blocking collectives, on_device(): kv_all = lax.all_gather(kv, 'seq', axis_index_groups=R_GROUPS)  52.7 us
    all_to_all x1, blocking collectives, on_device(): squares = lax.all_to_all(squares, 'head', 0, 0, tiled=True)  13.4 us
    all_to_all x1, waiting for transfers between devices, on_device(): lax.all_to_all(parts, 'seq', 0, 0, axis_index_groups=C_GROUPS, tiled=True)  11.9 us
    pallas_call x1, Pallas kernels, on_device(): pl.pallas_call(attend_kernel, out_shape=jax.ShapeDtypeStruct((NC, OROWS,...  8.18 us
    all_to_all x1, starting transfers between devices, on_device(): lax.all_to_all(q_parts, 'seq', 0, 0, axis_index_groups=C_GROUPS, tiled=True)  6.21 us
    all_to_all x1, starting transfers between devices, on_device(): lax.all_to_all(parts, 'seq', 0, 0, axis_index_groups=C_GROUPS, tiled=True)  4.68 us
  transfers between devices with their start and end apart: 2, of which 1 were waited for; matrix products, arithmetic and copies ran while one was open for 0% of the time, Pallas kernels for 2%

profile of v5, /device:TPU:1, one launch (start us, length us, event | category | flops | bytes accessed | tf_op | source)
XLA Modules:
  0.0 102.9 jit_solution(5030005704714846519)
XLA Ops:
  0.0 0.0 copy-start
  0.0 0.0 copy-start.1
  0.0 0.0 copy-start.3
  0.7 1.9 %query.1 = bf16[8,272,128]{2,1,0:T(8,128)(2,1)} custom-call(s32[1,8]{1,0:T(1,128)} %want_hbm.1, s32[1]{0:T(128)S(6)} %copy.11.fifo_hbm, bf16[256,128]{1,0:T(8,128)(2,1)} %bitcast.21), custom_call_target="tpu_custom_call" | custom-call | tf_op jit(solution)/shard_map/query/pallas_call | solution.py:265
  2.6 6.2 %all-to-all-start = ((bf16[8,272,128]{2,1,0:T(8,128)(2,1)}), bf16[8,272,128]{2,1,0:T(8,128)(2,1)S(1)}, u32[]{:S(2)}, u32[]{:S(2)}) async-start(bf16[8,272,128]{2,1,0:T(8,128)(2,1)} %query.1), calls=%async_computation | async-start | bytes 1114112 | tf_op jit(solution)/shard_map/all_to_all | solution.py:279
  8.8 0.0 copy-done
  8.8 0.0 copy-done.1
  8.8 0.0 copy-done.2
  8.8 0.0 copy-done.3
  8.8 1.8 %code.1 = s16[1040,128]{1,0:T(8,128)(2,1)S(1)} custom-call(bf16[256,128]{1,0:T(8,128)(2,1)S(1)} %bitcast.15, bf16[256,128]{1,0:T(8,128)(2,1)S(1)} %bitcast.16, bf16[256,128]{1,0:T(8,128)(2,1)S(1)} %bitcast.17, bf16[256,128]{1,0:T(8,128)(2,1)S(1)} %bitcast.18), custom_call_target="tpu_custom_call" | custom-call | tf_op jit(solution)/shard_map/code/pallas_call | solution.py:280
  10.6 0.1 pad_add_fusion.pos_ref
  10.7 52.7 %all-gather.2 = s16[8320,128]{1,0:T(8,128)(2,1)S(1)} all-gather(s16[1040,128]{1,0:T(8,128)(2,1)S(1)} %code.1), channel_id=2, replica_groups={{0,16,32,48,64,80,96,112},{8,24,40,56,72,88,104,120},{128,144,160,176,1..., dimensions={0}, use_global_device_ids=true | all-gather | bytes 2396160 | tf_op jit(solution)/shard_map/all_gather | solution.py:292
  63.4 0.0 all-to-all-done.q_ref
  63.5 8.2 %attend.1 = bf16[8,528,128]{2,1,0:T(8,128)(2,1)} custom-call(s32[3]{0:T(128)S(1)} %pad_add_fusion.pos_ref, bf16[8,272,128]{2,1,0:T(8,128)(2,1)S(1)} %all-to-all-done.q_ref, s16[8,1040,128]{2,1,0:T(8,128)(2,1)S(1)} %bitcast.14), custom_call_target="tpu_custom_call" | custom-call | tf_op jit(solution)/shard_map/attend/pallas_call | solution.py:293
  71.6 0.0 copy-start.5
  71.6 4.7 %all-to-all-start.1 = ((bf16[8,528,128]{2,1,0:T(8,128)(2,1)}), bf16[8,528,128]{2,1,0:T(8,128)(2,1)S(1)}, u32[]{:S(2)}, u32[]{:S(2)}) async-start(bf16[8,528,128]{2,1,0:T(8,128)(2,1)} %attend.1), calls=%async_computation.1 | async-start | bytes 2162688 | tf_op jit(solution)/shard_map/all_to_all | solution.py:302
  76.3 0.0 copy-done.5
  76.3 0.0 copy-start.4
  76.3 11.9 %all-to-all-done.1.part_ref = bf16[8,528,128]{2,1,0:T(8,128)(2,1)S(1)} async-done(((bf16[8,528,128]{2,1,0:T(8,128)(2,1)}), bf16[8,528,128]{2,1,0:T(8,128)(2,1)S(1)}, u32[]{:S(2)}, u32[]{:S(2)}) %all-to-all-start.1) | async-done | bytes 1081376 | tf_op jit(solution)/shard_map/all_to_all | solution.py:302
  88.3 0.1 broadcast_in_dim.2.gate_ref
  88.4 0.3 merge.1
  88.6 13.4 %all_to_all.21 = f32[8,1,128]{2,1,0:T(1,128)S(1)} all-to-all(f32[8,1,128]{2,1,0:T(1,128)S(1)} %bitcast.20), channel_id=1, replica_groups=mesh['seq'=64,'head'=8] {'head'}, dimensions={0} | all-to-all | bytes 8192 | tf_op jit(solution)/shard_map/all_to_all | solution.py:315
  102.0 0.0 copy-done.4
  102.0 0.9 final.1
  (2 shorter events, 0.0 us)
Async XLA Ops:
  0.0 8.8 %copy-start = (bf16[128,2,128]{2,1,0:T(2,128)(2,1)S(1)}, bf16[128,2,128]{2,1,0:T(2,128)(2,1)}, u32[]{:S(2)}) copy-start(bf16[128,2,128]{2,1,0:T(2,128)(2,1)} %param.10) | copy-start | bytes 196612
  0.0 8.8 %copy-start.1 = (bf16[128,2,128]{2,1,0:T(2,128)(2,1)S(1)}, bf16[128,2,128]{2,1,0:T(2,128)(2,1)}, u32[]{:S(2)}) copy-start(bf16[128,2,128]{2,1,0:T(2,128)(2,1)} %param.11) | copy-start | bytes 196612
  0.0 8.8 %copy-start.2 = (bf16[128,2,128]{2,1,0:T(2,128)(2,1)S(1)}, bf16[128,2,128]{2,1,0:T(2,128)(2,1)}, u32[]{:S(2)}) copy-start(bf16[128,2,128]{2,1,0:T(2,128)(2,1)} %param.12) | copy-start | bytes 196612
  0.0 8.8 %copy-start.3 = (bf16[128,2,128]{2,1,0:T(2,128)(2,1)S(1)}, bf16[128,2,128]{2,1,0:T(2,128)(2,1)}, u32[]{:S(2)}) copy-start(bf16[128,2,128]{2,1,0:T(2,128)(2,1)} %param.13) | copy-start | bytes 196612
  2.6 60.9 %all-to-all-start = ((bf16[8,272,128]{2,1,0:T(8,128)(2,1)}), bf16[8,272,128]{2,1,0:T(8,128)(2,1)S(1)}, u32[]{:S(2)}, u32[]{:S(2)}) async-start(bf16[8,272,128]{2,1,0:T(8,128)(2,1)} %query.1), calls=%async_computation | async-start | bytes 1114112 | tf_op jit(solution)/shard_map/all_to_all | solution.py:279
  71.6 4.7 %copy-start.5 = (f32[2]{0:T(128)S(1)}, f32[2]{0:T(128)}, u32[]{:S(2)}) copy-start(f32[2]{0:T(128)} %param.16) | copy-start | bytes 28
  71.6 16.7 %all-to-all-start.1 = ((bf16[8,528,128]{2,1,0:T(8,128)(2,1)}), bf16[8,528,128]{2,1,0:T(8,128)(2,1)S(1)}, u32[]{:S(2)}, u32[]{:S(2)}) async-start(bf16[8,528,128]{2,1,0:T(8,128)(2,1)} %attend.1), calls=%async_computation.1 | async-start | bytes 2162688 | tf_op jit(solution)/shard_map/all_to_all | solution.py:302
  76.3 25.7 %copy-start.4 = (f32[2,128]{1,0:T(2,128)S(1)}, f32[2,128]{1,0:T(2,128)}, u32[]{:S(2)}) copy-start(f32[2,128]{1,0:T(2,128)} %gain_ref.1) | copy-start | bytes 3076

commit v6 on v5

--- a/solution.py
+++ b/solution.py
@@ -79,9 +79,10 @@
             if i % 2:
                 block = jnp.transpose(block)
             peak = jnp.max(jnp.max(jnp.abs(block), 0, keepdims=True), 1, keepdims=True)
-            power = jnp.floor(14.999 - jnp.log2(jnp.maximum(peak, 1e-30)))
+            power = jnp.floor(14.997 - jnp.log2(jnp.maximum(peak, 1e-30)))
             power = jnp.broadcast_to(power, (1, TOK))
-            code = jnp.floor(block * jnp.exp2(power) + 0.5).astype(jnp.int32)
+            code = jnp.floor(block * jnp.exp2(power) + 0.5)
+            code = jnp.clip(code, -32767.0, 32767.0).astype(jnp.int32)
             kv_out[pl.ds((i * 2 + h) * TOK, TOK), :] = code.astype(jnp.int16)
             powers.append(power)
     powers.append(jnp.zeros((8, TOK), jnp.float32))
@@ -131,16 +132,17 @@
             top = jnp.full((8, 2 * TOK), FLOOR, jnp.float32)
             for i, r in enumerate(blocks):
                 s = mask(i, dot(keys_ref[at, pl.ds(tok_start(r), TOK), :], q_rows, NT))
+                s = s * LOG2_SCALE
                 s_ref[at, pl.ds(i * TOK, TOK), :] = s
                 top = jnp.maximum(top, jnp.max(s.reshape(TOK // 8, 8, 2 * TOK), 0))
-            tops.append(jnp.max(top, 0, keepdims=True) * LOG2_SCALE)
+            tops.append(jnp.max(top, 0, keepdims=True))
         for h in range(2):
             at = kind * 2 + h
             top = tops[h]
             acc = jnp.zeros((DH + 16, 2 * TOK), jnp.float32)
             for i in range(0, len(blocks), 2):
                 part = blocks[i : i + 2]
-                e = jnp.exp2(s_ref[at, pl.ds(i * TOK, len(part) * TOK), :] * LOG2_SCALE - top)
+                e = jnp.exp2(s_ref[at, pl.ds(i * TOK, len(part) * TOK), :] - top)
                 vals = jnp.concatenate([vals_ref[at, :, pl.ds(tok_start(r), TOK)] for r in part], 1)
                 acc = acc + dot(vals, e.astype(jnp.bfloat16), NN)
             total = jnp.maximum(acc[DH : DH + 1, :], 1e-30)

time: 103 us -> 103 us (level)
  starting transfers between devices: 10.9 us -> 13 us
  blocking collectives: 66.1 us -> 64.6 us
    all_to_all x1, starting transfers between devices: 4.68 us -> 6.74 us  [on_device(): lax.all_to_all(parts, 'seq', 0, 0, axis_index_groups=C_GROUPS, tiled=True)]
    all_gather x1, blocking collectives: 52.7 us -> 51.1 us  [on_device(): kv_all = lax.all_gather(kv, 'seq', axis_index_groups=R_GROUPS)]
where the time goes in v6:
time: 103 us
  blocking collectives  64.6 us (63%)
  starting transfers between devices  13 us (13%)
  Pallas kernels  12.5 us (12%)
  waiting for transfers between devices  12.1 us (12%)
    all_gather x1, blocking collectives, on_device(): kv_all = lax.all_gather(kv, 'seq', axis_index_groups=R_GROUPS)  51.1 us
    all_to_all x1, blocking collectives, on_device(): squares = lax.all_to_all(squares, 'head', 0, 0, tiled=True)  13.5 us
    all_to_all x1, waiting for transfers between devices, on_device(): lax.all_to_all(parts, 'seq', 0, 0, axis_index_groups=C_GROUPS, tiled=True)  12.1 us
    pallas_call x1, Pallas kernels, on_device(): pl.pallas_call(attend_kernel, out_shape=jax.ShapeDtypeStruct((NC, OROWS,...  7.64 us
    all_to_all x1, starting transfers between devices, on_device(): lax.all_to_all(parts, 'seq', 0, 0, axis_index_groups=C_GROUPS, tiled=True)  6.74 us
    all_to_all x1, starting transfers between devices, on_device(): lax.all_to_all(q_parts, 'seq', 0, 0, axis_index_groups=C_GROUPS, tiled=True)  6.21 us
  transfers between devices with their start and end apart: 2, of which 1 were waited for; matrix products, arithmetic and copies ran while one was open for 0% of the time, Pallas kernels for 2%

profile of v6, /device:TPU:1, one launch (start us, length us, event | category | flops | bytes accessed | tf_op | source)
XLA Modules:
  0.0 103.1 jit_solution(7031408645100125841)
XLA Ops:
  0.0 0.0 copy-start
  0.0 0.0 copy-start.1
  0.0 0.0 copy-start.2
  0.0 0.0 copy-start.3
  0.7 1.9 %query.1 = bf16[8,272,128]{2,1,0:T(8,128)(2,1)} custom-call(s32[1,8]{1,0:T(1,128)} %want_hbm.1, s32[1]{0:T(128)S(6)} %copy.11.fifo_hbm, bf16[256,128]{1,0:T(8,128)(2,1)} %bitcast.21), custom_call_target="tpu_custom_call" | custom-call | tf_op jit(solution)/shard_map/query/pallas_call | solution.py:267
  2.6 6.2 %all-to-all-start = ((bf16[8,272,128]{2,1,0:T(8,128)(2,1)}), bf16[8,272,128]{2,1,0:T(8,128)(2,1)S(1)}, u32[]{:S(2)}, u32[]{:S(2)}) async-start(bf16[8,272,128]{2,1,0:T(8,128)(2,1)} %query.1), calls=%async_computation | async-start | bytes 1114112 | tf_op jit(solution)/shard_map/all_to_all | solution.py:281
  8.8 0.0 copy-done
  8.8 0.0 copy-done.1
  8.8 0.0 copy-done.2
  8.8 0.0 copy-done.3
  8.8 1.8 %code.1 = s16[1040,128]{1,0:T(8,128)(2,1)S(1)} custom-call(bf16[256,128]{1,0:T(8,128)(2,1)S(1)} %bitcast.15, bf16[256,128]{1,0:T(8,128)(2,1)S(1)} %bitcast.16, bf16[256,128]{1,0:T(8,128)(2,1)S(1)} %bitcast.17, bf16[256,128]{1,0:T(8,128)(2,1)S(1)} %bitcast.18), custom_call_target="tpu_custom_call" | custom-call | tf_op jit(solution)/shard_map/code/pallas_call | solution.py:282
  10.6 0.1 pad_add_fusion.pos_ref
  10.7 51.1 %all-gather.2 = s16[8320,128]{1,0:T(8,128)(2,1)S(1)} all-gather(s16[1040,128]{1,0:T(8,128)(2,1)S(1)} %code.1), channel_id=2, replica_groups={{0,16,32,48,64,80,96,112},{8,24,40,56,72,88,104,120},{128,144,160,176,1..., dimensions={0}, use_global_device_ids=true | all-gather | bytes 2396160 | tf_op jit(solution)/shard_map/all_gather | solution.py:294
  61.9 0.0 all-to-all-done.q_ref
  61.9 7.6 %attend.1 = bf16[8,528,128]{2,1,0:T(8,128)(2,1)} custom-call(s32[3]{0:T(128)S(1)} %pad_add_fusion.pos_ref, bf16[8,272,128]{2,1,0:T(8,128)(2,1)S(1)} %all-to-all-done.q_ref, s16[8,1040,128]{2,1,0:T(8,128)(2,1)S(1)} %bitcast.14), custom_call_target="tpu_custom_call" | custom-call | tf_op jit(solution)/shard_map/attend/pallas_call | solution.py:295
  69.5 6.7 %all-to-all-start.1 = ((bf16[8,528,128]{2,1,0:T(8,128)(2,1)}), bf16[8,528,128]{2,1,0:T(8,128)(2,1)S(1)}, u32[]{:S(2)}, u32[]{:S(2)}) async-start(bf16[8,528,128]{2,1,0:T(8,128)(2,1)} %attend.1), calls=%async_computation.1 | async-start | bytes 2162688 | tf_op jit(solution)/shard_map/all_to_all | solution.py:304
  76.3 0.0 copy-done.5
  76.3 0.0 copy-start.4
  76.3 12.1 %all-to-all-done.1.part_ref = bf16[8,528,128]{2,1,0:T(8,128)(2,1)S(1)} async-done(((bf16[8,528,128]{2,1,0:T(8,128)(2,1)}), bf16[8,528,128]{2,1,0:T(8,128)(2,1)S(1)}, u32[]{:S(2)}, u32[]{:S(2)}) %all-to-all-start.1) | async-done | bytes 1081376 | tf_op jit(solution)/shard_map/all_to_all | solution.py:304
  88.4 0.1 broadcast_in_dim.2.gate_ref
  88.5 0.3 merge.1
  88.7 13.5 %all_to_all.21 = f32[8,1,128]{2,1,0:T(1,128)S(1)} all-to-all(f32[8,1,128]{2,1,0:T(1,128)S(1)} %bitcast.20), channel_id=1, replica_groups=mesh['seq'=64,'head'=8] {'head'}, dimensions={0} | all-to-all | bytes 8192 | tf_op jit(solution)/shard_map/all_to_all | solution.py:317
  102.2 0.0 copy-done.4
  102.2 0.9 final.1
  (2 shorter events, 0.0 us)
Async XLA Ops:
  0.0 8.8 %copy-start = (bf16[128,2,128]{2,1,0:T(2,128)(2,1)S(1)}, bf16[128,2,128]{2,1,0:T(2,128)(2,1)}, u32[]{:S(2)}) copy-start(bf16[128,2,128]{2,1,0:T(2,128)(2,1)} %param.10) | copy-start | bytes 196612
  0.0 8.8 %copy-start.1 = (bf16[128,2,128]{2,1,0:T(2,128)(2,1)S(1)}, bf16[128,2,128]{2,1,0:T(2,128)(2,1)}, u32[]{:S(2)}) copy-start(bf16[128,2,128]{2,1,0:T(2,128)(2,1)} %param.11) | copy-start | bytes 196612
  0.0 8.8 %copy-start.2 = (bf16[128,2,128]{2,1,0:T(2,128)(2,1)S(1)}, bf16[128,2,128]{2,1,0:T(2,128)(2,1)}, u32[]{:S(2)}) copy-start(bf16[128,2,128]{2,1,0:T(2,128)(2,1)} %param.12) | copy-start | bytes 196612
  0.0 8.8 %copy-start.3 = (bf16[128,2,128]{2,1,0:T(2,128)(2,1)S(1)}, bf16[128,2,128]{2,1,0:T(2,128)(2,1)}, u32[]{:S(2)}) copy-start(bf16[128,2,128]{2,1,0:T(2,128)(2,1)} %param.13) | copy-start | bytes 196612
  2.6 59.3 %all-to-all-start = ((bf16[8,272,128]{2,1,0:T(8,128)(2,1)}), bf16[8,272,128]{2,1,0:T(8,128)(2,1)S(1)}, u32[]{:S(2)}, u32[]{:S(2)}) async-start(bf16[8,272,128]{2,1,0:T(8,128)(2,1)} %query.1), calls=%async_computation | async-start | bytes 1114112 | tf_op jit(solution)/shard_map/all_to_all | solution.py:281
  69.5 6.7 %copy-start.5 = (f32[2]{0:T(128)S(1)}, f32[2]{0:T(128)}, u32[]{:S(2)}) copy-start(f32[2]{0:T(128)} %param.16) | copy-start | bytes 28
  69.5 18.9 %all-to-all-start.1 = ((bf16[8,528,128]{2,1,0:T(8,128)(2,1)}), bf16[8,528,128]{2,1,0:T(8,128)(2,1)S(1)}, u32[]{:S(2)}, u32[]{:S(2)}) async-start(bf16[8,528,128]{2,1,0:T(8,128)(2,1)} %attend.1), calls=%async_computation.1 | async-start | bytes 2162688 | tf_op jit(solution)/shard_map/all_to_all | solution.py:304
  76.3 26.0 %copy-start.4 = (f32[2,128]{1,0:T(2,128)S(1)}, f32[2,128]{1,0:T(2,128)}, u32[]{:S(2)}) copy-start(f32[2,128]{1,0:T(2,128)} %gain_ref.1) | copy-start | bytes 3076

commit v7 on v6

--- a/solution.py
+++ b/solution.py
@@ -38,7 +38,7 @@
     return jnp.where(col == source, 1.0, 0.0).astype(jnp.bfloat16)
 
 
-def query_kernel(want_hbm, fifo_hbm, q_hbm, q_out, want, fifo, q_in, sems):
+def query_kernel(want_hbm, fifo_hbm, q_hbm, q_hbm_out, want, fifo, q_in, q_split, rows, sems, out_sems):
     copies = [
         pltpu.make_async_copy(src, dst, sems.at[i])
         for i, (src, dst) in enumerate(((want_hbm, want), (fifo_hbm, fifo), (q_hbm, q_in)))
@@ -55,11 +55,16 @@
         for i in range(1, 8):
             chosen = chosen | (block == want[0, i])
         live = ((block - fifo[0] + BLOCKS) & (BLOCKS - 1)) >= EXPIRED
-        q_out[c, pl.ds(2 * TOK, 16), :] = jnp.where(chosen & live, 0.0, NEG).astype(jnp.bfloat16)
+        rows[c] = jnp.where(chosen & live, 0.0, NEG).astype(jnp.bfloat16)
+    sends = [pltpu.make_async_copy(rows, q_hbm_out.at[:, pl.ds(2 * TOK, 16), :], out_sems.at[NC])]
+    sends[0].start()
     copies[2].wait()
-    q_rows = dot(perm, q_in[...], NN).astype(jnp.bfloat16)
+    q_split[...] = dot(perm, q_in[...], NN).astype(jnp.bfloat16)
     for c in range(NC):
-        q_out[c, pl.ds(0, 2 * TOK), :] = q_rows
+        sends.append(pltpu.make_async_copy(q_split, q_hbm_out.at[c, pl.ds(0, 2 * TOK), :], out_sems.at[c]))
+        sends[-1].start()
+    for send in sends:
+        send.wait()
 
 
 def code_kernel(k_hbm, v_hbm, mk_hbm, mv_hbm, kv_out, rows_in, sems):
@@ -268,12 +273,15 @@
         query_kernel,
         out_shape=jax.ShapeDtypeStruct((NC, QROWS, DH), jnp.bfloat16),
         in_specs=[ANY] * 3,
-        out_specs=VMEM,
+        out_specs=ANY,
         scratch_shapes=[
             pltpu.SMEM((1, 8), jnp.int32),
             pltpu.SMEM((1,), jnp.int32),
             pltpu.VMEM((2 * TOK, DH), jnp.bfloat16),
+            pltpu.VMEM((2 * TOK, DH), jnp.bfloat16),
+            pltpu.VMEM((NC, 16, TOK), jnp.bfloat16),
             pltpu.SemaphoreType.DMA((3,)),
+            pltpu.SemaphoreType.DMA((NC + 1,)),
         ],
         compiler_params=WHOLE,
         name="query",

time: 103 us -> 103 us (level)
  starting transfers between devices: 13 us -> 9.91 us
  blocking collectives: 64.6 us -> 67.3 us
    all_gather x1, blocking collectives: 51.1 us -> 54.2 us  [on_device(): kv_all = lax.all_gather(kv, 'seq', axis_index_groups=R_GROUPS)]
    all_to_all x1, starting transfers between devices: 6.74 us -> 3.69 us  [on_device(): lax.all_to_all(parts, 'seq', 0, 0, axis_index_groups=C_GROUPS, tiled=True)]
where the time goes in v7:
time: 103 us
  blocking collectives  67.3 us (65%)
  Pallas kernels  12.6 us (12%)
  waiting for transfers between devices  12.4 us (12%)
  starting transfers between devices  9.91 us (10%)
    all_gather x1, blocking collectives, on_device(): kv_all = lax.all_gather(kv, 'seq', axis_index_groups=R_GROUPS)  54.2 us
    all_to_all x1, blocking collectives, on_device(): squares = lax.all_to_all(squares, 'head', 0, 0, tiled=True)  13.1 us
    all_to_all x1, waiting for transfers between devices, on_device(): lax.all_to_all(parts, 'seq', 0, 0, axis_index_groups=C_GROUPS, tiled=True)  12.4 us
    pallas_call x1, Pallas kernels, on_device(): pl.pallas_call(attend_kernel, out_shape=jax.ShapeDtypeStruct((NC, OROWS,...  7.63 us
    all_to_all x1, starting transfers between devices, on_device(): lax.all_to_all(q_parts, 'seq', 0, 0, axis_index_groups=C_GROUPS, tiled=True)  6.21 us
    all_to_all x1, starting transfers between devices, on_device(): lax.all_to_all(parts, 'seq', 0, 0, axis_index_groups=C_GROUPS, tiled=True)  3.69 us
  transfers between devices with their start and end apart: 2, of which 1 were waited for; matrix products, arithmetic and copies ran while one was open for 0% of the time, Pallas kernels for 2%

profile of v7, /device:TPU:1, one launch (start us, length us, event | category | flops | bytes accessed | tf_op | source)
XLA Modules:
  0.0 103.1 jit_solution(12502233681500774924)
XLA Ops:
  0.0 0.0 copy-start
  0.0 0.0 copy-start.1
  0.0 0.0 copy-start.2
  0.0 0.0 copy-start.3
  0.7 1.9 %query.1 = bf16[8,272,128]{2,1,0:T(8,128)(2,1)} custom-call(s32[1,8]{1,0:T(1,128)} %want_hbm.1, s32[1]{0:T(128)S(6)} %copy.11.fifo_hbm, bf16[256,128]{1,0:T(8,128)(2,1)} %bitcast.21), custom_call_target="tpu_custom_call" | custom-call | tf_op jit(solution)/shard_map/query/pallas_call | solution.py:272
  2.6 6.2 %all-to-all-start = ((bf16[8,272,128]{2,1,0:T(8,128)(2,1)}), bf16[8,272,128]{2,1,0:T(8,128)(2,1)S(1)}, u32[]{:S(2)}, u32[]{:S(2)}) async-start(bf16[8,272,128]{2,1,0:T(8,128)(2,1)} %query.1), calls=%async_computation | async-start | bytes 1114112 | tf_op jit(solution)/shard_map/all_to_all | solution.py:289
  8.9 0.0 copy-done
  8.9 0.0 copy-done.1
  8.9 0.0 copy-done.2
  8.9 0.0 copy-done.3
  8.9 1.8 %code.1 = s16[1040,128]{1,0:T(8,128)(2,1)S(1)} custom-call(bf16[256,128]{1,0:T(8,128)(2,1)S(1)} %bitcast.15, bf16[256,128]{1,0:T(8,128)(2,1)S(1)} %bitcast.16, bf16[256,128]{1,0:T(8,128)(2,1)S(1)} %bitcast.17, bf16[256,128]{1,0:T(8,128)(2,1)S(1)} %bitcast.18), custom_call_target="tpu_custom_call" | custom-call | tf_op jit(solution)/shard_map/code/pallas_call | solution.py:290
  10.7 0.1 pad_add_fusion.pos_ref
  10.8 54.2 %all-gather.2 = s16[8320,128]{1,0:T(8,128)(2,1)S(1)} all-gather(s16[1040,128]{1,0:T(8,128)(2,1)S(1)} %code.1), channel_id=2, replica_groups={{0,16,32,48,64,80,96,112},{8,24,40,56,72,88,104,120},{128,144,160,176,1..., dimensions={0}, use_global_device_ids=true | all-gather | bytes 2396160 | tf_op jit(solution)/shard_map/all_gather | solution.py:302
  65.0 0.0 all-to-all-done.q_ref
  65.0 7.6 %attend.1 = bf16[8,528,128]{2,1,0:T(8,128)(2,1)} custom-call(s32[3]{0:T(128)S(1)} %pad_add_fusion.pos_ref, bf16[8,272,128]{2,1,0:T(8,128)(2,1)S(1)} %all-to-all-done.q_ref, s16[8,1040,128]{2,1,0:T(8,128)(2,1)S(1)} %bitcast.14), custom_call_target="tpu_custom_call" | custom-call | tf_op jit(solution)/shard_map/attend/pallas_call | solution.py:303
  72.7 3.7 %all-to-all-start.1 = ((bf16[8,528,128]{2,1,0:T(8,128)(2,1)}), bf16[8,528,128]{2,1,0:T(8,128)(2,1)S(1)}, u32[]{:S(2)}, u32[]{:S(2)}) async-start(bf16[8,528,128]{2,1,0:T(8,128)(2,1)} %attend.1), calls=%async_computation.1 | async-start | bytes 2162688 | tf_op jit(solution)/shard_map/all_to_all | solution.py:312
  76.4 0.0 copy-done.5
  76.4 0.0 copy-start.4
  76.4 12.4 %all-to-all-done.1.part_ref = bf16[8,528,128]{2,1,0:T(8,128)(2,1)S(1)} async-done(((bf16[8,528,128]{2,1,0:T(8,128)(2,1)}), bf16[8,528,128]{2,1,0:T(8,128)(2,1)S(1)}, u32[]{:S(2)}, u32[]{:S(2)}) %all-to-all-start.1) | async-done | bytes 1081376 | tf_op jit(solution)/shard_map/all_to_all | solution.py:312
  88.8 0.1 broadcast_in_dim.2.gate_ref
  88.8 0.3 merge.1
  89.1 13.1 %all_to_all.21 = f32[8,1,128]{2,1,0:T(1,128)S(1)} all-to-all(f32[8,1,128]{2,1,0:T(1,128)S(1)} %bitcast.20), channel_id=1, replica_groups=mesh['seq'=64,'head'=8] {'head'}, dimensions={0} | all-to-all | bytes 8192 | tf_op jit(solution)/shard_map/all_to_all | solution.py:325
  102.2 0.0 copy-done.4
  102.2 0.9 final.1
  (2 shorter events, 0.0 us)
Async XLA Ops:
  0.0 8.9 %copy-start = (bf16[128,2,128]{2,1,0:T(2,128)(2,1)S(1)}, bf16[128,2,128]{2,1,0:T(2,128)(2,1)}, u32[]{:S(2)}) copy-start(bf16[128,2,128]{2,1,0:T(2,128)(2,1)} %param.10) | copy-start | bytes 196612
  0.0 8.9 %copy-start.1 = (bf16[128,2,128]{2,1,0:T(2,128)(2,1)S(1)}, bf16[128,2,128]{2,1,0:T(2,128)(2,1)}, u32[]{:S(2)}) copy-start(bf16[128,2,128]{2,1,0:T(2,128)(2,1)} %param.11) | copy-start | bytes 196612
  0.0 8.9 %copy-start.2 = (bf16[128,2,128]{2,1,0:T(2,128)(2,1)S(1)}, bf16[128,2,128]{2,1,0:T(2,128)(2,1)}, u32[]{:S(2)}) copy-start(bf16[128,2,128]{2,1,0:T(2,128)(2,1)} %param.12) | copy-start | bytes 196612
  0.0 8.9 %copy-start.3 = (bf16[128,2,128]{2,1,0:T(2,128)(2,1)S(1)}, bf16[128,2,128]{2,1,0:T(2,128)(2,1)}, u32[]{:S(2)}) copy-start(bf16[128,2,128]{2,1,0:T(2,128)(2,1)} %param.13) | copy-start | bytes 196612
  2.6 62.4 %all-to-all-start = ((bf16[8,272,128]{2,1,0:T(8,128)(2,1)}), bf16[8,272,128]{2,1,0:T(8,128)(2,1)S(1)}, u32[]{:S(2)}, u32[]{:S(2)}) async-start(bf16[8,272,128]{2,1,0:T(8,128)(2,1)} %query.1), calls=%async_computation | async-start | bytes 1114112 | tf_op jit(solution)/shard_map/all_to_all | solution.py:289
  72.7 3.7 %copy-start.5 = (f32[2]{0:T(128)S(1)}, f32[2]{0:T(128)}, u32[]{:S(2)}) copy-start(f32[2]{0:T(128)} %param.16) | copy-start | bytes 28
  72.7 16.1 %all-to-all-start.1 = ((bf16[8,528,128]{2,1,0:T(8,128)(2,1)}), bf16[8,528,128]{2,1,0:T(8,128)(2,1)S(1)}, u32[]{:S(2)}, u32[]{:S(2)}) async-start(bf16[8,528,128]{2,1,0:T(8,128)(2,1)} %attend.1), calls=%async_computation.1 | async-start | bytes 2162688 | tf_op jit(solution)/shard_map/all_to_all | solution.py:312
  76.4 25.8 %copy-start.4 = (f32[2,128]{1,0:T(2,128)S(1)}, f32[2,128]{1,0:T(2,128)}, u32[]{:S(2)}) copy-start(f32[2,128]{1,0:T(2,128)} %gain_ref.1) | copy-start | bytes 3076

commit v8 on v6

--- a/solution.py
+++ b/solution.py
@@ -181,7 +181,11 @@
 
             run(xq, 1, blocks, retrieved)
 
-        @pl.when(count <= 2)
+        @pl.when(count <= 1)
+        def _():
+            some(1)
+
+        @pl.when(count == 2)
         def _():
             some(2)
 

time: 103 us -> 104 us (level); the launches traced: 103 us -> 103 us
  no operation moved by 1% of the time
where the time goes in v8:
time: 104 us; the launch traced here: 103 us
  blocking collectives  64.6 us (62%)
  starting transfers between devices  12.8 us (12%)
  Pallas kernels  12.6 us (12%)
  waiting for transfers between devices  12.1 us (12%)
    all_gather x1, blocking collectives, on_device(): kv_all = lax.all_gather(kv, 'seq', axis_index_groups=R_GROUPS)  51.1 us
    all_to_all x1, blocking collectives, on_device(): squares = lax.all_to_all(squares, 'head', 0, 0, tiled=True)  13.5 us
    all_to_all x1, waiting for transfers between devices, on_device(): lax.all_to_all(parts, 'seq', 0, 0, axis_index_groups=C_GROUPS, tiled=True)  12.1 us
    pallas_call x1, Pallas kernels, on_device(): pl.pallas_call(attend_kernel, out_shape=jax.ShapeDtypeStruct((NC, OROWS,...  7.73 us
    all_to_all x1, starting transfers between devices, on_device(): lax.all_to_all(parts, 'seq', 0, 0, axis_index_groups=C_GROUPS, tiled=True)  6.59 us
    all_to_all x1, starting transfers between devices, on_device(): lax.all_to_all(q_parts, 'seq', 0, 0, axis_index_groups=C_GROUPS, tiled=True)  6.21 us
  transfers between devices with their start and end apart: 2, of which 1 were waited for; matrix products, arithmetic and copies ran while one was open for 0% of the time, Pallas kernels for 2%

profile of v8, /device:TPU:1, one launch (start us, length us, event | category | flops | bytes accessed | tf_op | source)
XLA Modules:
  0.0 103.1 jit_solution(14123906585238387028)
XLA Ops:
  0.0 0.0 copy-start
  0.0 0.0 copy-start.1
  0.0 0.0 copy-start.3
  0.7 1.9 %query.1 = bf16[8,272,128]{2,1,0:T(8,128)(2,1)} custom-call(s32[1,8]{1,0:T(1,128)} %want_hbm.1, s32[1]{0:T(128)S(6)} %copy.11.fifo_hbm, bf16[256,128]{1,0:T(8,128)(2,1)} %bitcast.21), custom_call_target="tpu_custom_call" | custom-call | tf_op jit(solution)/shard_map/query/pallas_call | solution.py:271
  2.6 6.2 %all-to-all-start = ((bf16[8,272,128]{2,1,0:T(8,128)(2,1)}), bf16[8,272,128]{2,1,0:T(8,128)(2,1)S(1)}, u32[]{:S(2)}, u32[]{:S(2)}) async-start(bf16[8,272,128]{2,1,0:T(8,128)(2,1)} %query.1), calls=%async_computation | async-start | bytes 1114112 | tf_op jit(solution)/shard_map/all_to_all | solution.py:285
  8.8 0.0 copy-done
  8.8 0.0 copy-done.1
  8.8 0.0 copy-done.2
  8.8 0.0 copy-done.3
  8.8 1.8 %code.1 = s16[1040,128]{1,0:T(8,128)(2,1)S(1)} custom-call(bf16[256,128]{1,0:T(8,128)(2,1)S(1)} %bitcast.15, bf16[256,128]{1,0:T(8,128)(2,1)S(1)} %bitcast.16, bf16[256,128]{1,0:T(8,128)(2,1)S(1)} %bitcast.17, bf16[256,128]{1,0:T(8,128)(2,1)S(1)} %bitcast.18), custom_call_target="tpu_custom_call" | custom-call | tf_op jit(solution)/shard_map/code/pallas_call | solution.py:286
  10.6 0.1 pad_add_fusion.pos_ref
  10.7 51.1 %all-gather.2 = s16[8320,128]{1,0:T(8,128)(2,1)S(1)} all-gather(s16[1040,128]{1,0:T(8,128)(2,1)S(1)} %code.1), channel_id=2, replica_groups={{0,16,32,48,64,80,96,112},{8,24,40,56,72,88,104,120},{128,144,160,176,1..., dimensions={0}, use_global_device_ids=true | all-gather | bytes 2396160 | tf_op jit(solution)/shard_map/all_gather | solution.py:298
  61.9 0.0 all-to-all-done.q_ref
  61.9 7.7 %attend.1 = bf16[8,528,128]{2,1,0:T(8,128)(2,1)} custom-call(s32[3]{0:T(128)S(1)} %pad_add_fusion.pos_ref, bf16[8,272,128]{2,1,0:T(8,128)(2,1)S(1)} %all-to-all-done.q_ref, s16[8,1040,128]{2,1,0:T(8,128)(2,1)S(1)} %bitcast.14), custom_call_target="tpu_custom_call" | custom-call | tf_op jit(solution)/shard_map/attend/pallas_call | solution.py:299
  69.6 0.0 copy-start.5
  69.6 6.6 %all-to-all-start.1 = ((bf16[8,528,128]{2,1,0:T(8,128)(2,1)}), bf16[8,528,128]{2,1,0:T(8,128)(2,1)S(1)}, u32[]{:S(2)}, u32[]{:S(2)}) async-start(bf16[8,528,128]{2,1,0:T(8,128)(2,1)} %attend.1), calls=%async_computation.1 | async-start | bytes 2162688 | tf_op jit(solution)/shard_map/all_to_all | solution.py:308
  76.2 0.0 copy-done.5
  76.2 0.0 copy-start.4
  76.2 12.1 %all-to-all-done.1.part_ref = bf16[8,528,128]{2,1,0:T(8,128)(2,1)S(1)} async-done(((bf16[8,528,128]{2,1,0:T(8,128)(2,1)}), bf16[8,528,128]{2,1,0:T(8,128)(2,1)S(1)}, u32[]{:S(2)}, u32[]{:S(2)}) %all-to-all-start.1) | async-done | bytes 1081376 | tf_op jit(solution)/shard_map/all_to_all | solution.py:308
  88.3 0.1 broadcast_in_dim.2.gate_ref
  88.4 0.3 merge.1
  88.7 13.5 %all_to_all.21 = f32[8,1,128]{2,1,0:T(1,128)S(1)} all-to-all(f32[8,1,128]{2,1,0:T(1,128)S(1)} %bitcast.20), channel_id=1, replica_groups=mesh['seq'=64,'head'=8] {'head'}, dimensions={0} | all-to-all | bytes 8192 | tf_op jit(solution)/shard_map/all_to_all | solution.py:321
  102.2 0.0 copy-done.4
  102.2 0.9 final.1
  (2 shorter events, 0.0 us)
Async XLA Ops:
  0.0 8.8 %copy-start = (bf16[128,2,128]{2,1,0:T(2,128)(2,1)S(1)}, bf16[128,2,128]{2,1,0:T(2,128)(2,1)}, u32[]{:S(2)}) copy-start(bf16[128,2,128]{2,1,0:T(2,128)(2,1)} %param.10) | copy-start | bytes 196612
  0.0 8.8 %copy-start.1 = (bf16[128,2,128]{2,1,0:T(2,128)(2,1)S(1)}, bf16[128,2,128]{2,1,0:T(2,128)(2,1)}, u32[]{:S(2)}) copy-start(bf16[128,2,128]{2,1,0:T(2,128)(2,1)} %param.11) | copy-start | bytes 196612
  0.0 8.8 %copy-start.2 = (bf16[128,2,128]{2,1,0:T(2,128)(2,1)S(1)}, bf16[128,2,128]{2,1,0:T(2,128)(2,1)}, u32[]{:S(2)}) copy-start(bf16[128,2,128]{2,1,0:T(2,128)(2,1)} %param.12) | copy-start | bytes 196612
  0.0 8.8 %copy-start.3 = (bf16[128,2,128]{2,1,0:T(2,128)(2,1)S(1)}, bf16[128,2,128]{2,1,0:T(2,128)(2,1)}, u32[]{:S(2)}) copy-start(bf16[128,2,128]{2,1,0:T(2,128)(2,1)} %param.13) | copy-start | bytes 196612
  2.6 59.3 %all-to-all-start = ((bf16[8,272,128]{2,1,0:T(8,128)(2,1)}), bf16[8,272,128]{2,1,0:T(8,128)(2,1)S(1)}, u32[]{:S(2)}, u32[]{:S(2)}) async-start(bf16[8,272,128]{2,1,0:T(8,128)(2,1)} %query.1), calls=%async_computation | async-start | bytes 1114112 | tf_op jit(solution)/shard_map/all_to_all | solution.py:285
  69.6 6.6 %copy-start.5 = (f32[2]{0:T(128)S(1)}, f32[2]{0:T(128)}, u32[]{:S(2)}) copy-start(f32[2]{0:T(128)} %param.16) | copy-start | bytes 28
  69.6 18.7 %all-to-all-start.1 = ((bf16[8,528,128]{2,1,0:T(8,128)(2,1)}), bf16[8,528,128]{2,1,0:T(8,128)(2,1)S(1)}, u32[]{:S(2)}, u32[]{:S(2)}) async-start(bf16[8,528,128]{2,1,0:T(8,128)(2,1)} %attend.1), calls=%async_computation.1 | async-start | bytes 2162688 | tf_op jit(solution)/shard_map/all_to_all | solution.py:308
  76.2 26.0 %copy-start.4 = (f32[2,128]{1,0:T(2,128)S(1)}, f32[2,128]{1,0:T(2,128)}, u32[]{:S(2)}) copy-start(f32[2,128]{1,0:T(2,128)} %gain_ref.1) | copy-start | bytes 3076
